TPU v7x, 256 devices: a whole 4x4x8 slice. The times are simulated.
256 devices in a mesh: outer: 16 (over x_lo, z), inner: 16 (over y, x_hi, core).
Axes of the slice: x: 4 (x_hi: 2, x_lo: 2; x = x_hi * 2 + x_lo), y: 4, z: 8, core: 2. Of those that a mesh axis runs over, the one named last changes fastest.
Arguments:
- images: float32 [131072, 1152], P(('outer', 'inner')), may hold values from -0.5 to 0.5
- texts: float32 [131072, 1152], P(('outer', 'inner')), may hold values from -0.5 to 0.5
- partner: int32 [256, 512], P(('outer', 'inner')), may hold values from 0 to 511, each once within a row
- logit_scale: float32 [1], replicated, may hold values from 8 to 12
- logit_bias: float32 [1], replicated, may hold values from -8 to -6
Outputs:
- image_grad: float32 [131072, 1152], P(('outer', 'inner'))
- text_grad: float32 [131072, 1152], P(('outer', 'inner'))
Inputs may be any that keep to these rules, and one draw needn't show every extreme that they name: Each row of partner is a permutation of the 512 rows of its block: every image pairs with exactly one text of its own block and every text with exactly one image.
All inputs are finite; a program needn't handle non-finite values.
Results may differ from a plain program's by a relative error of at most 0.00011.
Values sent between devices are 32-bit elements; how exact they have to be, the bound alone decides.
No kernel may reach another device: no remote copies, remote signals or barrier semaphores. Data moves between devices by JAX's collectives and lax.ppermute only.
A program may use at most 64 MiB of HBM per device.

v0:
```python
import jax
import jax.numpy as jnp
from jax import lax
from jax.experimental import pallas as pl
from jax.experimental.pallas import tpu as pltpu
from jax.sharding import PartitionSpec as P

REST = 4
TILE = 256
F32, BF16 = jnp.float32, jnp.bfloat16
ROW_ROW = (((1,), (1,)), ((), ()))
ROW_COL = (((1,), (0,)), ((), ()))
COL_COL = (((0,), (0,)), ((), ()))
VMEM = pl.BlockSpec(memory_space=pltpu.VMEM)
SMEM = pl.BlockSpec(memory_space=pltpu.SMEM)


def split(x):
    high = x.astype(BF16)
    return high, (x - high.astype(F32)).astype(BF16)


def mm(a, b, dims):
    def one(p, q):
        return lax.dot_general(p, q, dims, preferred_element_type=F32)

    return one(a[0], b[0]) + (one(a[0], b[1]) + one(a[1], b[0]))


def weights(image, text, scale, bias):
    logits = scale * mm(image, text, ROW_ROW) + bias
    return scale * jax.nn.sigmoid(logits)


def split_rows(src, high, low):
    def body(k, carry):
        rows = pl.ds(k * 128, 128)
        high[rows, :], low[rows, :] = split(src[rows, :])
        return carry

    lax.fori_loop(0, src.shape[0] // 128, body, 0)


def own_kernel(scale_ref, bias_ref, images, texts, partner, image_grad, text_grad, ih, il, th, tl):
    scale, bias = scale_ref[0], bias_ref[0]
    split_rows(texts, th, tl)
    split_rows(images, ih, il)
    text = (th[...], tl[...])
    for k in range(images.shape[0] // TILE):
        rows = pl.ds(k * TILE, TILE)
        image = (ih[rows, :], il[rows, :])
        w = weights(image, text, scale, bias)
        columns = lax.broadcasted_iota(jnp.int32, w.shape, 1)
        w = split(w - jnp.where(partner[rows, :] == columns, scale, 0.0))
        image_grad[rows, :] = mm(w, text, ROW_COL)
        term = mm(w, image, COL_COL)
        text_grad[...] = term if k == 0 else text_grad[...] + term


def piece_body(scale, bias, piece, th, tl, nh, nl, back, next_sum, ph, pq, wh, wl, next_in):
    image = split(piece[...])
    ph[...], pq[...] = image
    text = (nh[...], nl[...])
    w = split(weights(image, text, scale, bias))
    term = mm(w, image, COL_COL)
    next_sum[...] = term if next_in is None else next_in[...] + term
    total = mm(w, text, ROW_COL)
    text = (th[...], tl[...])
    w = split(weights(image, text, scale, bias))
    wh[...], wl[...] = w
    back[...] = total + mm(w, text, ROW_COL)


def first_kernel(scale_ref, bias_ref, piece, th, tl, text_next, back, next_sum, ph, pq, wh, wl, nh, nl):
    split_rows(text_next, nh, nl)
    piece_body(scale_ref[0], bias_ref[0], piece, th, tl, nh, nl, back, next_sum, ph, pq, wh, wl, None)


def next_kernel(scale_ref, bias_ref, ih, il, nh, nl, grad_in, next_in, image_grad, next_sum):
    scale, bias = scale_ref[0], bias_ref[0]
    text = (nh[...], nl[...])
    for k in range(ih.shape[0] // TILE):
        rows = pl.ds(k * TILE, TILE)
        image = (ih[rows, :], il[rows, :])
        w = split(weights(image, text, scale, bias))
        image_grad[rows, :] = grad_in[rows, :] + mm(w, text, ROW_COL)
        next_sum[...] = (next_in if k == 0 else next_sum)[...] + mm(w, image, COL_COL)


def last_kernel(scale_ref, bias_ref, piece, th, tl, nh, nl, next_in, back, next_sum, ph, pq, wh, wl):
    piece_body(scale_ref[0], bias_ref[0], piece, th, tl, nh, nl, back, next_sum, ph, pq, wh, wl, next_in)


def rest_kernel(scale_ref, bias_ref, text_in, grad_in, back, *refs):
    text_grad, image_grad = refs[-2:]
    size = back.shape[0]
    image_grad[:size, :] = grad_in[:size, :] + back[...]
    image_grad[size:, :] = grad_in[size:, :]
    total = text_in[...]
    for k in range(0, len(refs) - 2, 4):
        ph, pq, wh, wl = refs[k : k + 4]
        total = total + mm((wh[...], wl[...]), (ph[...], pq[...]), COL_COL)
    text_grad[...] = total


def call(kernel, outs, args, aliases, flops):
    return pl.pallas_call(
        kernel,
        out_shape=[jax.ShapeDtypeStruct(s, d) for s, d in outs],
        in_specs=[SMEM, SMEM] + [VMEM] * (len(args) - 2),
        out_specs=[VMEM] * len(outs),
        input_output_aliases=aliases,
        cost_estimate=pl.CostEstimate(flops=flops, bytes_accessed=2**20, transcendentals=0),
        compiler_params=pltpu.CompilerParams(vmem_limit_bytes=30 * 2**20),
    )(*args)


def shifted(array, axis, by):
    size = lax.axis_size(axis)
    return lax.ppermute(array, axis, [(i, (i + by) % size) for i in range(size)])


def shards(images, texts, partner, scale, bias):
    rows, width = images.shape
    size = rows // 2
    block, half = ((rows, width), F32), ((rows, width), BF16)
    part = [((size, width), F32), block, ((size, width), BF16), ((size, width), BF16)]
    part = part + [((size, rows), BF16), ((size, rows), BF16)]
    work = 6 * rows * rows * width
    text_next = shifted(texts, "inner", -1)
    first = shifted(images[:size], "outer", 1)
    last = shifted(images[size:], "outer", 1)
    image_grad, text_grad, ih, il, th, tl = call(
        own_kernel,
        [block, block, half, half, half, half],
        [scale, bias, images, texts, partner.reshape(rows, 1)],
        {},
        3 * work,
    )
    back0, next_sum, *kept0, nh, nl = call(
        first_kernel, part + [half, half], [scale, bias, first, th, tl, text_next], {}, 3 * work
    )
    back0 = shifted(back0, "outer", -1)
    image_grad, next_sum = call(
        next_kernel, [block, block], [scale, bias, ih, il, nh, nl, image_grad, next_sum], {6: 0, 7: 1}, 3 * work
    )
    back1, next_sum, *kept1 = call(
        last_kernel, part, [scale, bias, last, th, tl, nh, nl, next_sum], {7: 1}, 3 * work
    )
    next_back = shifted(next_sum, "inner", 1)
    back1 = shifted(back1, "outer", -1)
    text_grad, image_grad = call(
        rest_kernel,
        [block, block],
        [scale, bias, text_grad, image_grad, back0, *kept0, *kept1],
        {2: 0, 3: 1},
        REST * work,
    )
    image_grad = image_grad.at[size:].add(back1)
    return image_grad, text_grad + next_back


def solution(mesh):
    placed = (
        P(("outer", "inner"), None),
        P(("outer", "inner"), None),
        P(("outer", "inner"), None),
        P(),
        P(),
    )
    return jax.shard_map(
        shards,
        mesh=mesh,
        in_specs=placed,
        out_specs=(P(("outer", "inner"), None), P(("outer", "inner"), None)),
        check_vma=False,
    )
```

profile of v0, /device:TPU:224, one launch (start us, length us, event | category | flops | bytes accessed | tf_op | source)
XLA Modules:
  0.0 151.2 jit_solution(4484342190891601878)
XLA Ops:
  0.6 0.0 copy-start
  0.6 0.0 copy-start.2
  0.6 5.0 %collective-permute-start.1 = (f32[512,1152]{1,0:T(8,128)}, f32[512,1152]{1,0:T(8,128)}, u32[]{:S(2)}, u32[]{:S(2)}) collective-permute-start(f32[512,1152]{1,0:T(8,128)} %texts.1), channel_id=1, source_target_pairs={{0,15},{1,0},{2,1},{3,2},{4,3},{5,4},{6,5},{7,6},{8,7},{9,8},{10,9... | collective-permute-start | bytes 7077896 | tf_op jit(solution)/shard_map/ppermute | solution.py:120
  5.6 3.2 %fusion = (f32[256,1152]{1,0:T(8,128)}, f32[256,1152]{1,0:T(8,128)}) fusion(f32[512,1152]{1,0:T(8,128)} %images.1), kind=kLoop, calls=%fused_computation.1 | loop fusion | bytes 4718592 | tf_op jit(solution)/shard_map/slice | solution.py:132
  8.9 0.0 collective-permute-start
  8.9 0.0 collective-permute-start.3
  10.2 0.0 copy-done.2
  10.2 0.1 copy.12.partner
  10.3 0.0 copy-done
  10.3 0.0 copy-start.1
  10.3 1.7 %copy-done.1 = f32[512,1152]{1,0:T(8,128)S(1)} copy-done((f32[512,1152]{1,0:T(8,128)S(1)}, f32[512,1152]{1,0:T(8,128)}, u32[]{:S(2)}) %copy-start.1) | copy-done | bytes 2359320
  12.0 9.7 %shard_map.68 = (f32[512,1152]{1,0:T(8,128)}, f32[512,1152]{1,0:T(8,128)S(1)}, bf16[512,1152]{1,0:T(8,128)(2,1)S(1)}, bf16[512,1152]{1,0:T(8,128)(2,1)S(1)}, bf1...) custom-call(f32[1]{0:T(128)S(6)} %copy.19.scale_ref, f32[1]{0:T(128)S(6)} %copy.20.bias_ref, ...), custom_call_target="tpu_custom_call" | custom-call | flops 5435817984 | bytes 1048576 | tf_op jit(solution)/shard_map/pallas_call | solution.py:107
  21.8 16.3 %collective-permute-done.piece = f32[256,1152]{1,0:T(8,128)} collective-permute-done((f32[256,1152]{1,0:T(8,128)}, f32[256,1152]{1,0:T(8,128)}, u32[]{:S(2)}, u32[]{:S(2)}) %collective-permute-start) | collective-permute-done | bytes 1179680 | tf_op jit(solution)/shard_map/ppermute | solution.py:120
  38.1 0.0 collective-permute-done.1.text_next
  38.1 8.4 %shard_map.69 = (f32[256,1152]{1,0:T(8,128)S(1)}, f32[512,1152]{1,0:T(8,128)S(1)}, bf16[256,1152]{1,0:T(8,128)(2,1)S(1)}, bf16[256,1152]{1,0:T(8,128)(2,1)S(1)},...) custom-call(f32[1]{0:T(128)S(6)} %copy.19.scale_ref, ...), custom_call_target="tpu_custom_call" | custom-call | flops 5435817984 | bytes 1048576 | tf_op jit(solution)/shard_map/pallas_call | solution.py:107
  46.5 1.3 collective-permute-start.2
  47.8 12.1 %shard_map.70 = (f32[512,1152]{1,0:T(8,128)}, f32[512,1152]{1,0:T(8,128)S(1)}) custom-call(f32[1]{0:T(128)S(6)} %copy.19.scale_ref, f32[1]{0:T(128)S(6)} %copy.20.bias_ref, bf16[512,1152]{1,0:T(8,128)(2,1)S(1)} %get-tuple-element.39.ih, bf16[512,1152]{1,0:T(8,128)(2,1)S(1)} %get-tuple-element.40.il, ...), custom_call_target="tpu_custom_call", output_to_operand_aliasing={{0}: (6, {}), {1}: (7, {})} | custom-call | flops 5435817984 | bytes 1048576 | tf_op jit(solution)/shard_map/pallas_call | solution.py:107
  59.9 0.0 collective-permute-done.3.piece
  59.9 7.1 %shard_map.71 = (f32[256,1152]{1,0:T(8,128)S(1)}, f32[512,1152]{1,0:T(8,128)S(1)}, bf16[256,1152]{1,0:T(8,128)(2,1)S(1)}, bf16[256,1152]{1,0:T(8,128)(2,1)S(1)},...) custom-call(f32[1]{0:T(128)S(6)} %copy.19.scale_ref, ...), custom_call_target="tpu_custom_call", output_to_operand_aliasing={{1}: (7, {})} | custom-call | flops 5435817984 | bytes 1048576 | tf_op jit(solution)/shard_map/pallas_call | solution.py:107
  67.0 0.1 collective-permute-start.5
  67.1 1.3 collective-permute-start.4
  68.5 47.5 %collective-permute-done.2.back = f32[256,1152]{1,0:T(8,128)S(1)} collective-permute-done((f32[256,1152]{1,0:T(8,128)S(1)}, f32[256,1152]{1,0:T(8,128)S(1)}, u32[]{:S(2)}, u32[]{:S(2)}) %collective-permute-start.2) | collective-permute-done | bytes 1179680 | tf_op jit(solution)/shard_map/ppermute | solution.py:120
  116.0 5.6 %shard_map.72 = (f32[512,1152]{1,0:T(8,128)S(1)}, f32[512,1152]{1,0:T(8,128)}) custom-call(f32[1]{0:T(128)S(6)} %copy.19.scale_ref, f32[1]{0:T(128)S(6)} %copy.20.bias_ref, f32[512,1152]{1,0:T(8,128)S(1)} %get-tuple-element.38.text_in, f32[512,1152]{1,0:T(8,128)} %get-tuple-element.47.grad_in, ...), custom_call_target="tpu_custom_call", output_to_operand_aliasing={{0}: (2, {}), {1}: (3, {})} | custom-call | flops 7247757312 | bytes 1048576 | tf_op jit(solution)/shard_map/pallas_call | solution.py:107
  121.6 18.2 %collective-permute-done.4 = f32[256,1152]{1,0:T(8,128)S(1)} collective-permute-done((f32[256,1152]{1,0:T(8,128)S(1)}, f32[256,1152]{1,0:T(8,128)S(1)}, u32[]{:S(2)}, u32[]{:S(2)}) %collective-permute-start.4) | collective-permute-done | bytes 1179680 | tf_op jit(solution)/shard_map/ppermute | solution.py:120
  139.8 2.4 %add_dynamic-update-slice_fusion = f32[512,1152]{1,0:T(8,128)} fusion(f32[512,1152]{1,0:T(8,128)} %get-tuple-element.58, f32[256,1152]{1,0:T(8,128)S(1)} %collective-permute-done.4), kind=kLoop, calls=%fused_computation | loop fusion | flops 294912 | bytes 3538944 | tf_op jit(solution)/shard_map/scatter-add | solution.py:159
  142.2 7.4 %collective-permute-done.5 = f32[512,1152]{1,0:T(8,128)S(1)} collective-permute-done((f32[512,1152]{1,0:T(8,128)S(1)}, f32[512,1152]{1,0:T(8,128)S(1)}, u32[]{:S(2)}, u32[]{:S(2)}) %collective-permute-start.5) | collective-permute-done | bytes 2359328 | tf_op jit(solution)/shard_map/ppermute | solution.py:120
  149.5 1.6 %add.11 = f32[512,1152]{1,0:T(8,128)} add(f32[512,1152]{1,0:T(8,128)S(1)} %get-tuple-element.60, f32[512,1152]{1,0:T(8,128)S(1)} %collective-permute-done.5) | non-fusion elementwise | flops 589824 | bytes 7077888 | tf_op jit(solution)/shard_map/add | solution.py:160
Async XLA Ops:
  0.6 9.7 %copy-start = (f32[512,1152]{1,0:T(8,128)S(1)}, f32[512,1152]{1,0:T(8,128)}, u32[]{:S(2)}) copy-start(f32[512,1152]{1,0:T(8,128)} %images.1) | copy-start | bytes 7077892
  0.6 9.5 %copy-start.2 = (s32[1,512]{1,0:T(1,128)S(1)}, s32[1,512]{1,0:T(1,128)}, u32[]{:S(2)}) copy-start(s32[1,512]{1,0:T(1,128)} %param.9) | copy-start | bytes 6148
  0.6 37.4 %collective-permute-start.1 = (f32[512,1152]{1,0:T(8,128)}, f32[512,1152]{1,0:T(8,128)}, u32[]{:S(2)}, u32[]{:S(2)}) collective-permute-start(f32[512,1152]{1,0:T(8,128)} %texts.1), channel_id=1, source_target_pairs={{0,15},{1,0},{2,1},{3,2},{4,3},{5,4},{6,5},{7,6},{8,7},{9,8},{10,9... | collective-permute-start | bytes 7077896 | tf_op jit(solution)/shard_map/ppermute | solution.py:120
  8.9 29.2 %collective-permute-start = (f32[256,1152]{1,0:T(8,128)}, f32[256,1152]{1,0:T(8,128)}, u32[]{:S(2)}, u32[]{:S(2)}) collective-permute-start(f32[256,1152]{1,0:T(8,128)} %get-tuple-element.63), channel_id=1, source_target_pairs={{0,16},{16,32},{32,48},{48,64},{64,80},{80,96},{96,112},{112,128},... | collective-permute-start | bytes 3538952 | tf_op jit(solution)/shard_map/ppermute | solution.py:120
  8.9 51.0 %collective-permute-start.3 = (f32[256,1152]{1,0:T(8,128)}, f32[256,1152]{1,0:T(8,128)}, u32[]{:S(2)}, u32[]{:S(2)}) collective-permute-start(f32[256,1152]{1,0:T(8,128)} %get-tuple-element.62), channel_id=1, source_target_pairs={{0,16},{16,32},{32,48},{48,64},{64,80},{80,96},{96,112},{112,128},... | collective-permute-start | bytes 3538952 | tf_op jit(solution)/shard_map/ppermute | solution.py:120
  10.3 1.7 %copy-start.1 = (f32[512,1152]{1,0:T(8,128)S(1)}, f32[512,1152]{1,0:T(8,128)}, u32[]{:S(2)}) copy-start(f32[512,1152]{1,0:T(8,128)} %texts.1) | copy-start | bytes 7077892
  46.5 69.5 %collective-permute-start.2 = (f32[256,1152]{1,0:T(8,128)S(1)}, f32[256,1152]{1,0:T(8,128)S(1)}, u32[]{:S(2)}, u32[]{:S(2)}) collective-permute-start(f32[256,1152]{1,0:T(8,128)S(1)} %get-tuple-element.48), channel_id=1, source_target_pairs={{0,240},{16,0},{32,16},{48,32},{64,48},{80,64},{96,80},{112,96},{1... | collective-permute-start | bytes 3538952 | tf_op jit(solution)/shard_map/ppermute | solution.py:120
  67.0 82.5 %collective-permute-start.5 = (f32[512,1152]{1,0:T(8,128)S(1)}, f32[512,1152]{1,0:T(8,128)S(1)}, u32[]{:S(2)}, u32[]{:S(2)}) collective-permute-start(f32[512,1152]{1,0:T(8,128)S(1)} %get-tuple-element.61), channel_id=1, source_target_pairs={{0,1},{1,2},{2,3},{3,4},{4,5},{5,6},{6,7},{7,8},{8,9},{9,10},{10,1... | collective-permute-start | bytes 7077896 | tf_op jit(solution)/shard_map/ppermute | solution.py:120
  67.1 72.7 %collective-permute-start.4 = (f32[256,1152]{1,0:T(8,128)S(1)}, f32[256,1152]{1,0:T(8,128)S(1)}, u32[]{:S(2)}, u32[]{:S(2)}) collective-permute-start(f32[256,1152]{1,0:T(8,128)S(1)} %get-tuple-element.59), channel_id=1, source_target_pairs={{0,240},{16,0},{32,16},{48,32},{64,48},{80,64},{96,80},{112,96},{1... | collective-permute-start | bytes 3538952 | tf_op jit(solution)/shard_map/ppermute | solution.py:120
where the time goes:
time: 152 us; the launch traced here: 151 us
  waiting for transfers between devices  89.4 us (59%)
  Pallas kernels  43 us (28%)
  starting transfers between devices  7.73 us (5%)
  local copies, waits for them, and re-layouts  5.03 us (3%)
  other arithmetic  4.04 us (3%)
  between operations  2.01 us (1%)
    ppermute x6, waiting for transfers between devices, shifted(): lax.ppermute(array, axis, [(i, (i + by) % size) for i in range(size)])  89.4 us
    pallas_call x5, Pallas kernels, call(): pl.pallas_call(kernel, out_shape=[jax.ShapeDtypeStruct(s, d) for s, d in...  43 us
    ppermute x6, starting transfers between devices, shifted(): lax.ppermute(array, axis, [(i, (i + by) % size) for i in range(size)])  7.73 us
    slice x1, local copies, waits for them, and re-layouts, shards(): last = shifted(images[size:], 'outer', 1)  3.21 us
  transfers between devices with their start and end apart: 6, of which 4 were waited for; matrix products, arithmetic and copies ran while one was open for 4% of the time, Pallas kernels for 28%

commit v1 on v0

v1 whole, which is shorter than its diff:
```python
import functools

import jax
import jax.numpy as jnp
from jax import lax
from jax.experimental import pallas as pl
from jax.experimental.pallas import tpu as pltpu
from jax.sharding import PartitionSpec as P

OWN, AHEAD, FIRST, LAST, NEXT, REST_TEXT, REST_IMAGE = 3, 1, 1, 2, 3, 1, 40
TILE = 256
F32, BF16 = jnp.float32, jnp.bfloat16
ROW_ROW = (((1,), (1,)), ((), ()))
ROW_COL = (((1,), (0,)), ((), ()))
COL_COL = (((0,), (0,)), ((), ()))
VMEM = pl.BlockSpec(memory_space=pltpu.VMEM)
SMEM = pl.BlockSpec(memory_space=pltpu.SMEM)
HBM = pl.BlockSpec(memory_space=pltpu.HBM)


def split(x):
    high = x.astype(BF16)
    return high, (x - high.astype(F32)).astype(BF16)


def mm(a, b, dims):
    def one(p, q):
        return lax.dot_general(p, q, dims, preferred_element_type=F32)

    return one(a[0], b[0]) + (one(a[0], b[1]) + one(a[1], b[0]))


def weights(image, text, scale, bias):
    logits = scale * mm(image, text, ROW_ROW) + bias
    return scale * jax.nn.sigmoid(logits)


def split_rows(src, high, low):
    def body(k, carry):
        rows = pl.ds(k * 128, 128)
        high[rows, :], low[rows, :] = split(src[rows, :])
        return carry

    lax.fori_loop(0, src.shape[0] // 128, body, 0)


def store_halves(value, low, high):
    cut = low.shape[0]
    low[...], high[...] = value[:cut], value[cut:]


def own_kernel(scale_ref, bias_ref, images, texts, partner, image_grad, text_grad, ih, il, th, tl):
    scale, bias = scale_ref[0], bias_ref[0]
    split_rows(texts, th, tl)
    split_rows(images, ih, il)
    text = (th[...], tl[...])
    for k in range(images.shape[0] // TILE):
        rows = pl.ds(k * TILE, TILE)
        image = (ih[rows, :], il[rows, :])
        w = weights(image, text, scale, bias)
        columns = lax.broadcasted_iota(jnp.int32, w.shape, 1)
        w = split(w - jnp.where(partner[rows, :] == columns, scale, 0.0))
        image_grad[rows, :] = mm(w, text, ROW_COL)
        term = mm(w, image, COL_COL)
        text_grad[...] = term if k == 0 else text_grad[...] + term


def ahead_kernel(scale_ref, bias_ref, piece, th, tl, ph, pq, wh, wl, total):
    image, text = split(piece[...]), (th[...], tl[...])
    ph[...], pq[...] = image
    w = split(weights(image, text, scale_ref[0], bias_ref[0]))
    wh[...], wl[...] = w
    total[...] = mm(w, text, ROW_COL)


def first_kernel(scale_ref, bias_ref, ph, pq, text_next, total, straight, across, vh, vl, nh, nl):
    split_rows(text_next, nh, nl)
    image, text = (ph[...], pq[...]), (nh[...], nl[...])
    w = split(weights(image, text, scale_ref[0], bias_ref[0]))
    vh[...], vl[...] = w
    store_halves(total[...] + mm(w, text, ROW_COL), straight, across)


def last_kernel(scale_ref, bias_ref, piece, th, tl, nh, nl, straight, across, ph, pq, wh, wl, vh, vl):
    image = split(piece[...])
    ph[...], pq[...] = image
    text = (th[...], tl[...])
    w = split(weights(image, text, scale_ref[0], bias_ref[0]))
    wh[...], wl[...] = w
    total = mm(w, text, ROW_COL)
    text = (nh[...], nl[...])
    w = split(weights(image, text, scale_ref[0], bias_ref[0]))
    vh[...], vl[...] = w
    store_halves(total + mm(w, text, ROW_COL), straight, across)


def next_kernel(scale_ref, bias_ref, ih, il, nh, nl, *refs):
    early, late, uh, ul = refs[-4:]
    text = (nh[...], nl[...])
    for k in range(ih.shape[0] // TILE):
        rows = pl.ds(k * TILE, TILE)
        w = split(weights((ih[rows, :], il[rows, :]), text, scale_ref[0], bias_ref[0]))
        uh[rows, :], ul[rows, :] = w
    total = mm((uh[...], ul[...]), (ih[...], il[...]), COL_COL)
    for ph, pq, vh, vl in (refs[:4], refs[4:8]):
        total = total + mm((vh[...], vl[...]), (ph[...], pq[...]), COL_COL)
    store_halves(total, early, late)


def rest_text_kernel(scale_ref, bias_ref, text_in, *refs):
    total = text_in[...]
    for ph, pq, wh, wl in (refs[:4], refs[4:8]):
        total = total + mm((wh[...], wl[...]), (ph[...], pq[...]), COL_COL)
    store_halves(total, refs[-2], refs[-1])


def rest_image_kernel(scale_ref, bias_ref, grad_in, uh, ul, nh, nl, back0, back1, out, held0, held1, done0, done1, sems):
    cut, size = back0.shape[0], grad_in.shape[0] // 2
    copies = []
    for k, (back, held, done) in enumerate(((back0, held0, done0), (back1, held1, done1))):
        rows = pl.ds(k * size, size)
        total = grad_in[rows, :] + mm((uh[rows, :], ul[rows, :]), (nh[...], nl[...]), ROW_COL)
        done[...] = total[:cut] + back[...]
        copies.append(pltpu.make_async_copy(done, out.at[pl.ds(k * size, cut), :], sems.at[k]))
        copies[-1].start()
        held[...] = total[cut:]
    for copy in copies:
        copy.wait()


def place_kernel(start, held, back, *refs):
    out, buffer, sem = refs[-3:]
    buffer[...] = held[...] + back[...]
    copy = pltpu.make_async_copy(buffer, out.at[pl.ds(start, buffer.shape[0]), :], sem)
    copy.start()
    copy.wait()


def place(held, back, start, out, shape):
    given = [] if out is None else [out]
    return pl.pallas_call(
        functools.partial(place_kernel, start),
        out_shape=jax.ShapeDtypeStruct(shape, F32),
        in_specs=[VMEM, VMEM] + [HBM] * len(given),
        out_specs=HBM,
        scratch_shapes=[pltpu.VMEM(held.shape, F32), pltpu.SemaphoreType.DMA],
        input_output_aliases={2: 0} if given else {},
        compiler_params=pltpu.CompilerParams(vmem_limit_bytes=16 * 2**20),
    )(held, back, *given)


def call(kernel, outs, args, aliases, flops, scratch=(), far=0):
    return pl.pallas_call(
        kernel,
        out_shape=[jax.ShapeDtypeStruct(s, d) for s, d in outs],
        in_specs=[SMEM, SMEM] + [VMEM] * (len(args) - 2),
        out_specs=[HBM] * far + [VMEM] * (len(outs) - far),
        scratch_shapes=list(scratch),
        input_output_aliases=aliases,
        cost_estimate=pl.CostEstimate(flops=flops, bytes_accessed=2**20, transcendentals=0),
        compiler_params=pltpu.CompilerParams(vmem_limit_bytes=30 * 2**20),
    )(*args)


def shifted(array, axis, by):
    size = lax.axis_size(axis)
    return lax.ppermute(array, axis, [(i, (i + by) % size) for i in range(size)])


def crossed(array, at, keep=True):
    half = lax.axis_size("outer") // 2
    pairs = [(i, (i + half) % (2 * half)) for i in range(2 * half) if i % half == at % half]
    if keep:
        pairs += [(i, i) for i in range(2 * half) if i % half != at % half]
    return lax.ppermute(array, "outer", pairs)


def turned(array, by):
    half = lax.axis_size("outer") // 2
    pairs = [(i, i // half * half + (i + by) % half) for i in range(2 * half)]
    return lax.ppermute(array, "outer", pairs)


def tied(*arrays):
    return lax.optimization_barrier(arrays)


def shards(images, texts, partner, scale, bias):
    rows, width = images.shape
    size = rows // 2
    block, half, piece = ((rows, width), F32), ((rows, width), BF16), ((size, width), F32)
    quarter = ((size // 2, width), F32)
    ends = [piece, piece]
    low, w_low = ((size, width), BF16), ((size, rows), BF16)
    work = 6 * rows * rows * width
    last = images[size:]
    last, images, texts = tied(last, images, texts)
    other = crossed(last, -1, False)
    text_next = shifted(texts, "inner", -1)
    first = shifted(images[:size], "outer", 1)
    image_grad, text_grad, ih, il, th, tl = call(
        own_kernel,
        [block, block, half, half, half, half],
        [scale, bias, images, texts, partner.reshape(rows, 1)],
        {},
        OWN * work,
    )
    other, th = tied(other, th)
    outer = lax.axis_size("outer") // 2
    last = jnp.where(lax.axis_index("outer") % outer == outer - 1, other, last)
    last = turned(last, 1)
    *kept0, wh, wl, total = call(
        ahead_kernel, [low, low, w_low, w_low, piece], [scale, bias, first, th, tl], {}, AHEAD * work
    )
    straight0, across0, vh, vl, nh, nl = call(
        first_kernel,
        [quarter, quarter, w_low, w_low, half, half],
        [scale, bias, *kept0, text_next, total],
        {},
        FIRST * work,
    )
    straight0 = shifted(straight0, "outer", -1)
    across0 = crossed(across0, 0)
    mine0, next0 = [*kept0, wh, wl], [*kept0, vh, vl]
    straight1, across1, *kept1 = call(
        last_kernel,
        [quarter, quarter, low, low, w_low, w_low, w_low, w_low],
        [scale, bias, last, th, tl, nh, nl],
        {},
        LAST * work,
    )
    straight1 = shifted(straight1, "outer", -1)
    across1 = crossed(across1, 0)
    mine1, next1 = kept1[:4], kept1[:2] + kept1[4:]
    early, late, uh, ul = call(
        next_kernel,
        [*ends, ((rows, rows), BF16), ((rows, rows), BF16)],
        [scale, bias, ih, il, nh, nl, *next0, *next1],
        {},
        NEXT * work,
    )
    early, late = shifted(early, "inner", 1), shifted(late, "inner", 1)
    uh, text_grad, across0 = tied(uh, text_grad, across0)
    across0 = turned(across0, -1)
    text0, text1 = call(rest_text_kernel, ends, [scale, bias, text_grad, *mine0, *mine1], {}, REST_TEXT * work)
    text0, uh, across1, straight0, straight1 = tied(text0, uh, across1, straight0, straight1)
    across1 = turned(across1, -1)
    image_grad, image0, image1 = call(
        rest_image_kernel,
        [block, quarter, quarter],
        [scale, bias, image_grad, uh, ul, nh, nl, straight0, straight1],
        {},
        REST_IMAGE * work,
        [pltpu.VMEM((size // 2, width), F32)] * 2 + [pltpu.SemaphoreType.DMA((2,))],
        1,
    )
    text_grad = place(text0, early, 0, None, images.shape)
    image_grad = place(image0, across0, size // 2, image_grad, images.shape)
    image_grad = place(image1, across1, size + size // 2, image_grad, images.shape)
    image_grad, late = tied(image_grad, late)
    text_grad = place(text1, late, size, text_grad, images.shape)
    return image_grad, text_grad


def solution(mesh):
    placed = (
        P(("outer", "inner"), None),
        P(("outer", "inner"), None),
        P(("outer", "inner"), None),
        P(),
        P(),
    )
    return jax.shard_map(
        shards,
        mesh=mesh,
        in_specs=placed,
        out_specs=(P(("outer", "inner"), None), P(("outer", "inner"), None)),
        check_vma=False,
    )
```

time: 152 us -> 126 us (0.83)
  waiting for transfers between devices: 89.4 us -> 65 us
  starting transfers between devices: 7.73 us -> 13.2 us
  Pallas kernels: 43 us -> 38 us
  other arithmetic: 4.04 us -> 1.4 us
    ppermute x6, waiting for transfers between devices: 89.4 us -> 35.9 us  [shifted(): lax.ppermute(array, axis, [(i, (i + by) % size) for i in range(size)])]
    ppermute x0 -> x6, waiting for transfers between devices: none -> 29.1 us  [the longest x3 20.8 us: turned(): return lax.ppermute(array, 'outer', pairs)]
    pallas_call x5 -> x7, Pallas kernels: 43 us -> 34 us  [call(): pl.pallas_call(kernel, out_shape=[jax.ShapeDtypeStruct(s, d) for s, d in...]
    ppermute x0 -> x6, starting transfers between devices: none -> 5.26 us  [the longest x3 4.92 us: crossed(): return lax.ppermute(array, 'outer', pairs)]
    pallas_call x0 -> x4, Pallas kernels: none -> 4.05 us  [place(): pl.pallas_call(functools.partial(place_kernel, start), out_shape=jax.Shap...]
    scatter-add x1 -> x0, other arithmetic: 2.4 us -> none  [shards(): image_grad = image_grad.at[size:].add(back1)]
    add x1 -> x0, other arithmetic: 1.64 us -> none  [shards(): return (image_grad, text_grad + next_back)]
    slice x1 -> x2, local copies, waits for them, and re-layouts: 3.21 us -> 3.6 us  [the longest x1 2.51 us: shards(): last = images[size:]]
  transfers between devices with their start and end apart: 6 -> 12, of which waited for: 4 -> 7; matrix products, arithmetic and copies ran while one was open for 4% -> 2% of each run, Pallas kernels for 28% -> 28%
where the time goes in v1:
time: 126 us; the launch traced here: 125 us
  waiting for transfers between devices  65 us (52%)
  Pallas kernels  38 us (30%)
  starting transfers between devices  13.2 us (10%)
  local copies, waits for them, and re-layouts  5.42 us (4%)
  between operations  2.29 us (2%)
  other arithmetic  1.4 us (1%)
    ppermute x6, waiting for transfers between devices, shifted(): lax.ppermute(array, axis, [(i, (i + by) % size) for i in range(size)])  35.9 us
    pallas_call x7, Pallas kernels, call(): pl.pallas_call(kernel, out_shape=[jax.ShapeDtypeStruct(s, d) for s, d in...  34 us
    ppermute x3, waiting for transfers between devices, turned(): return lax.ppermute(array, 'outer', pairs)  20.8 us
    ppermute x3, waiting for transfers between devices, crossed(): return lax.ppermute(array, 'outer', pairs)  8.3 us
    ppermute x6, starting transfers between devices, shifted(): lax.ppermute(array, axis, [(i, (i + by) % size) for i in range(size)])  7.98 us
    ppermute x3, starting transfers between devices, crossed(): return lax.ppermute(array, 'outer', pairs)  4.92 us
    pallas_call x4, Pallas kernels, place(): pl.pallas_call(functools.partial(place_kernel, start), out_shape=jax.Shap...  4.05 us
  transfers between devices with their start and end apart: 12, of which 7 were waited for; matrix products, arithmetic and copies ran while one was open for 2% of the time, Pallas kernels for 28%

profile of v1, /device:TPU:224, one launch (start us, length us, event | category | flops | bytes accessed | tf_op | source)
XLA Modules:
  0.0 125.4 jit_solution(14041135719142735809)
XLA Ops:
  0.6 2.5 %slice.6 = f32[256,1152]{1,0:T(8,128)} slice(f32[512,1152]{1,0:T(8,128)} %images), slice={[256:512], [0:1152]} | slice | bytes 2359296 | tf_op jit(solution)/shard_map/slice | solution.py:196
  3.2 3.5 %collective-permute-start.1 = (f32[256,1152]{1,0:T(8,128)}, f32[256,1152]{1,0:T(8,128)}, u32[]{:S(2)}, u32[]{:S(2)}) collective-permute-start(f32[256,1152]{1,0:T(8,128)} %slice.6), channel_id=1, source_target_pairs={{112,240},{240,112},{113,241},{241,113},{114,242},{242,114},{115,2... | collective-permute-start | bytes 3538952 | tf_op jit(solution)/shard_map/ppermute | solution.py:175
  6.7 4.4 %collective-permute-start.2 = (f32[512,1152]{1,0:T(8,128)}, f32[512,1152]{1,0:T(8,128)}, u32[]{:S(2)}, u32[]{:S(2)}) collective-permute-start(f32[512,1152]{1,0:T(8,128)} %texts), channel_id=1, source_target_pairs={{0,15},{1,0},{2,1},{3,2},{4,3},{5,4},{6,5},{7,6},{8,7},{9,8},{10,9... | collective-permute-start | bytes 7077896 | tf_op jit(solution)/shard_map/ppermute | solution.py:167
  11.1 1.1 slice.7
  13.5 0.1 copy.10.partner
  13.7 1.7 %copy-done.1 = f32[512,1152]{1,0:T(8,128)S(1)} copy-done((f32[512,1152]{1,0:T(8,128)S(1)}, f32[512,1152]{1,0:T(8,128)}, u32[]{:S(2)}) %copy-start.1) | copy-done | bytes 2359320
  15.3 9.6 %shard_map.68 = (f32[512,1152]{1,0:T(8,128)S(1)}, f32[512,1152]{1,0:T(8,128)S(1)}, bf16[512,1152]{1,0:T(8,128)(2,1)S(1)}, bf16[512,1152]{1,0:T(8,128)(2,1)S(1)},...) custom-call(f32[1]{0:T(128)S(6)} %copy.14.scale_ref, f32[1]{0:T(128)S(6)} %copy.15.bias_ref, ...), custom_call_target="tpu_custom_call" | custom-call | flops 5435817984 | bytes 1048576 | tf_op jit(solution)/shard_map/pallas_call | solution.py:153
  24.9 8.3 %collective-permute-done.1 = f32[256,1152]{1,0:T(8,128)} collective-permute-done((f32[256,1152]{1,0:T(8,128)}, f32[256,1152]{1,0:T(8,128)}, u32[]{:S(2)}, u32[]{:S(2)}) %collective-permute-start.1) | collective-permute-done | bytes 1179680 | tf_op jit(solution)/shard_map/ppermute | solution.py:175
  33.2 1.4 %broadcast_select_fusion = f32[256,1152]{1,0:T(8,128)S(1)} fusion(f32[256,1152]{1,0:T(8,128)} %collective-permute-done.1, f32[256,1152]{1,0:T(8,128)} %slice.6, pred[]{:T(512)S(6)} %eq.5), kind=kLoop, calls=%fused_computation | loop fusion | flops 294912 | bytes 3538945 | tf_op jit(solution)/shard_map/jit(_where)/select_n | solution.py:210
  34.6 0.3 collective-permute-start.3
  34.9 1.7 %collective-permute-done.piece = f32[256,1152]{1,0:T(8,128)} collective-permute-done((f32[256,1152]{1,0:T(8,128)}, f32[256,1152]{1,0:T(8,128)}, u32[]{:S(2)}, u32[]{:S(2)}) %collective-permute-start) | collective-permute-done | bytes 1179680 | tf_op jit(solution)/shard_map/ppermute | solution.py:167
  36.5 3.6 %shard_map.69 = (bf16[256,1152]{1,0:T(8,128)(2,1)S(1)}, bf16[256,1152]{1,0:T(8,128)(2,1)S(1)}, bf16[256,512]{1,0:T(8,128)(2,1)S(1)}, bf16[256,512]{1,0:T(8,128)(2,1)S(1)}, f32[256,1152]{1,0:T(8,128)S(1)}) custom-call(f32[1]{0:T(128)S(6)} %copy.14.scale_ref, f32[1]{0:T(128)S(6)} %copy.15.bias_ref, f32[256,1152]{1,0:T(8,128)} %collective-permute-done.piece, ...), custom_call_target="tpu_custom_call" | custom-call | flops 1811939328 | bytes 1048576 | tf_op jit(solution)/shard_map/pallas_call | solution.py:153
  40.2 17.3 %collective-permute-done.2.text_next = f32[512,1152]{1,0:T(8,128)} collective-permute-done((f32[512,1152]{1,0:T(8,128)}, f32[512,1152]{1,0:T(8,128)}, u32[]{:S(2)}, u32[]{:S(2)}) %collective-permute-start.2) | collective-permute-done | bytes 2359328 | tf_op jit(solution)/shard_map/ppermute | solution.py:167
  57.5 4.5 %shard_map.70 = (f32[128,1152]{1,0:T(8,128)S(1)}, f32[128,1152]{1,0:T(8,128)S(1)}, bf16[256,512]{1,0:T(8,128)(2,1)S(1)}, bf16[256,512]{1,0:T(8,128)(2,1)S(1)}, b...) custom-call(f32[1]{0:T(128)S(6)} %copy.14.scale_ref, f32[1]{0:T(128)S(6)} %copy.15.bias_ref, ...), custom_call_target="tpu_custom_call" | custom-call | flops 1811939328 | bytes 1048576 | tf_op jit(solution)/shard_map/pallas_call | solution.py:153
  61.9 0.7 collective-permute-start.4
  62.6 0.1 collective-permute-start.6
  62.7 4.6 %shard_map.71 = (f32[128,1152]{1,0:T(8,128)S(1)}, f32[128,1152]{1,0:T(8,128)S(1)}, bf16[256,1152]{1,0:T(8,128)(2,1)S(1)}, bf16[256,1152]{1,0:T(8,128)(2,1)S(1)},...) custom-call(f32[1]{0:T(128)S(6)} %copy.14.scale_ref, ...), custom_call_target="tpu_custom_call" | custom-call | flops 3623878656 | bytes 1048576 | tf_op jit(solution)/shard_map/pallas_call | solution.py:153
  67.3 0.7 collective-permute-start.5
  68.0 0.3 collective-permute-start.7
  68.3 6.5 %shard_map.72 = (f32[256,1152]{1,0:T(8,128)S(1)}, f32[256,1152]{1,0:T(8,128)S(1)}, bf16[512,512]{1,0:T(8,128)(2,1)S(1)}, bf16[512,512]{1,0:T(8,128)(2,1)S(1)}) custom-call(f32[1]{0:T(128)S(6)} %copy.14.scale_ref, f32[1]{0:T(128)S(6)} %copy.15.bias_ref, bf16[512,1152]{1,0:T(8,128)(2,1)S(1)} %get-tuple-element.54.ih, ...), custom_call_target="tpu_custom_call" | custom-call | flops 5435817984 | bytes 1048576 | tf_op jit(solution)/shard_map/pallas_call | solution.py:153
  74.8 3.1 %collective-permute-start.10 = (f32[256,1152]{1,0:T(8,128)S(1)}, f32[256,1152]{1,0:T(8,128)S(1)}, u32[]{:S(2)}, u32[]{:S(2)}) collective-permute-start(f32[256,1152]{1,0:T(8,128)S(1)} %get-tuple-element.94), channel_id=1, source_target_pairs={{0,1},{1,2},{2,3},{3,4},{4,5},{5,6},{6,7},{7,8},{8,9},{9,10},{10,1... | collective-permute-start | bytes 3538952 | tf_op jit(solution)/shard_map/ppermute | solution.py:167
  77.9 0.1 collective-permute-start.11
  78.0 2.2 %shard_map.73 = (f32[256,1152]{1,0:T(8,128)S(1)}, f32[256,1152]{1,0:T(8,128)S(1)}) custom-call(f32[1]{0:T(128)S(6)} %copy.14.scale_ref, f32[1]{0:T(128)S(6)} %copy.15.bias_ref, f32[512,1152]{1,0:T(8,128)S(1)} %get-tuple-element.75.text_in, bf16[256,1152]{1,0:T(8,128)(2,1)S(1)} %get-tuple-element.60.ph.refs_0_, ...), custom_call_target="tpu_custom_call" | custom-call | flops 1811939328 | bytes 1048576 | tf_op jit(solution)/shard_map/pallas_call | solution.py:153
  80.4 11.9 %collective-permute-done.7.back1 = f32[128,1152]{1,0:T(8,128)S(1)} collective-permute-done((f32[128,1152]{1,0:T(8,128)S(1)}, f32[128,1152]{1,0:T(8,128)S(1)}, u32[]{:S(2)}, u32[]{:S(2)}) %collective-permute-start.7) | collective-permute-done | bytes 589856 | tf_op jit(solution)/shard_map/ppermute | solution.py:167
  92.3 3.0 %shard_map.74 = (f32[512,1152]{1,0:T(8,128)}, f32[128,1152]{1,0:T(8,128)S(1)}, f32[128,1152]{1,0:T(8,128)S(1)}) custom-call(f32[1]{0:T(128)S(6)} %copy.14.scale_ref, f32[1]{0:T(128)S(6)} %copy.15.bias_ref, f32[512,1152]{1,0:T(8,128)S(1)} %get-tuple-element.53.grad_in, bf16[512,512]{1,0:T(8,128)(2,1)S(1)} %get-tuple-element.85.uh, ...), custom_call_target="tpu_custom_call" | custom-call | flops 72477573120 | bytes 1048576 | tf_op jit(solution)/shard_map/pallas_call | solution.py:153
  95.3 9.1 %collective-permute-done.9.back = f32[128,1152]{1,0:T(8,128)S(1)} collective-permute-done((f32[128,1152]{1,0:T(8,128)S(1)}, f32[128,1152]{1,0:T(8,128)S(1)}, u32[]{:S(2)}, u32[]{:S(2)}) %collective-permute-start.9) | collective-permute-done | bytes 589856 | tf_op jit(solution)/shard_map/ppermute | solution.py:181
  104.4 0.9 shard_map.75.refs_0_
  105.3 11.7 %collective-permute-done.8.back = f32[128,1152]{1,0:T(8,128)S(1)} collective-permute-done((f32[128,1152]{1,0:T(8,128)S(1)}, f32[128,1152]{1,0:T(8,128)S(1)}, u32[]{:S(2)}, u32[]{:S(2)}) %collective-permute-start.8) | collective-permute-done | bytes 589856 | tf_op jit(solution)/shard_map/ppermute | solution.py:181
  117.0 0.9 shard_map.76
  117.9 5.0 %collective-permute-done.11.back = f32[256,1152]{1,0:T(8,128)S(1)} collective-permute-done((f32[256,1152]{1,0:T(8,128)S(1)}, f32[256,1152]{1,0:T(8,128)S(1)}, u32[]{:S(2)}, u32[]{:S(2)}) %collective-permute-start.11) | collective-permute-done | bytes 1179680 | tf_op jit(solution)/shard_map/ppermute | solution.py:167
  122.9 1.1 shard_map.77.refs_0_
  124.1 1.1 shard_map.78
  (13 shorter events, 0.1 us)
Async XLA Ops:
  0.6 10.5 %copy-start = (f32[512,1152]{1,0:T(8,128)S(1)}, f32[512,1152]{1,0:T(8,128)}, u32[]{:S(2)}) copy-start(f32[512,1152]{1,0:T(8,128)} %images) | copy-start | bytes 7077892
  3.1 10.3 %copy-start.2 = (s32[1,512]{1,0:T(1,128)S(1)}, s32[1,512]{1,0:T(1,128)}, u32[]{:S(2)}) copy-start(s32[1,512]{1,0:T(1,128)} %param.7) | copy-start | bytes 6148
  3.2 30.0 %collective-permute-start.1 = (f32[256,1152]{1,0:T(8,128)}, f32[256,1152]{1,0:T(8,128)}, u32[]{:S(2)}, u32[]{:S(2)}) collective-permute-start(f32[256,1152]{1,0:T(8,128)} %slice.6), channel_id=1, source_target_pairs={{112,240},{240,112},{113,241},{241,113},{114,242},{242,114},{115,2... | collective-permute-start | bytes 3538952 | tf_op jit(solution)/shard_map/ppermute | solution.py:175
  6.7 50.8 %collective-permute-start.2 = (f32[512,1152]{1,0:T(8,128)}, f32[512,1152]{1,0:T(8,128)}, u32[]{:S(2)}, u32[]{:S(2)}) collective-permute-start(f32[512,1152]{1,0:T(8,128)} %texts), channel_id=1, source_target_pairs={{0,15},{1,0},{2,1},{3,2},{4,3},{5,4},{6,5},{7,6},{8,7},{9,8},{10,9... | collective-permute-start | bytes 7077896 | tf_op jit(solution)/shard_map/ppermute | solution.py:167
  12.2 24.4 %collective-permute-start = (f32[256,1152]{1,0:T(8,128)}, f32[256,1152]{1,0:T(8,128)}, u32[]{:S(2)}, u32[]{:S(2)}) collective-permute-start(f32[256,1152]{1,0:T(8,128)} %slice.7), channel_id=1, source_target_pairs={{0,16},{16,32},{32,48},{48,64},{64,80},{80,96},{96,112},{112,128},... | collective-permute-start | bytes 3538952 | tf_op jit(solution)/shard_map/ppermute | solution.py:167
  13.7 1.7 %copy-start.1 = (f32[512,1152]{1,0:T(8,128)S(1)}, f32[512,1152]{1,0:T(8,128)}, u32[]{:S(2)}) copy-start(f32[512,1152]{1,0:T(8,128)} %texts) | copy-start | bytes 7077892
  34.6 28.1 %collective-permute-start.3 = (f32[256,1152]{1,0:T(8,128)S(1)}, f32[256,1152]{1,0:T(8,128)S(1)}, u32[]{:S(2)}, u32[]{:S(2)}) collective-permute-start(f32[256,1152]{1,0:T(8,128)S(1)} %broadcast_select_fusion), channel_id=1, source_target_pairs={{0,16},{16,32},{32,48},{48,64},{64,80},{80,96},{96,112},{112,0},{1... | collective-permute-start | bytes 3538952 | tf_op jit(solution)/shard_map/ppermute | solution.py:181
  61.9 16.0 %collective-permute-start.4 = (f32[128,1152]{1,0:T(8,128)S(1)}, f32[128,1152]{1,0:T(8,128)S(1)}, u32[]{:S(2)}, u32[]{:S(2)}) collective-permute-start(f32[128,1152]{1,0:T(8,128)S(1)} %get-tuple-element.74), channel_id=1, source_target_pairs={{0,128},{128,0},{16,16},{32,32},{48,48},{64,64},{80,80},{96,96},{1... | collective-permute-start | bytes 1769480 | tf_op jit(solution)/shard_map/ppermute | solution.py:175
  62.6 17.6 %collective-permute-start.6 = (f32[128,1152]{1,0:T(8,128)S(1)}, f32[128,1152]{1,0:T(8,128)S(1)}, u32[]{:S(2)}, u32[]{:S(2)}) collective-permute-start(f32[128,1152]{1,0:T(8,128)S(1)} %get-tuple-element.83), channel_id=1, source_target_pairs={{0,240},{16,0},{32,16},{48,32},{64,48},{80,64},{96,80},{112,96},{1... | collective-permute-start | bytes 1769480 | tf_op jit(solution)/shard_map/ppermute | solution.py:167
  67.3 13.0 %collective-permute-start.5 = (f32[128,1152]{1,0:T(8,128)S(1)}, f32[128,1152]{1,0:T(8,128)S(1)}, u32[]{:S(2)}, u32[]{:S(2)}) collective-permute-start(f32[128,1152]{1,0:T(8,128)S(1)} %get-tuple-element.82), channel_id=1, source_target_pairs={{0,128},{128,0},{16,16},{32,32},{48,48},{64,64},{80,80},{96,96},{1... | collective-permute-start | bytes 1769480 | tf_op jit(solution)/shard_map/ppermute | solution.py:175
  68.0 24.3 %collective-permute-start.7 = (f32[128,1152]{1,0:T(8,128)S(1)}, f32[128,1152]{1,0:T(8,128)S(1)}, u32[]{:S(2)}, u32[]{:S(2)}) collective-permute-start(f32[128,1152]{1,0:T(8,128)S(1)} %get-tuple-element.84), channel_id=1, source_target_pairs={{0,240},{16,0},{32,16},{48,32},{64,48},{80,64},{96,80},{112,96},{1... | collective-permute-start | bytes 1769480 | tf_op jit(solution)/shard_map/ppermute | solution.py:167
  74.8 43.1 %collective-permute-start.10 = (f32[256,1152]{1,0:T(8,128)S(1)}, f32[256,1152]{1,0:T(8,128)S(1)}, u32[]{:S(2)}, u32[]{:S(2)}) collective-permute-start(f32[256,1152]{1,0:T(8,128)S(1)} %get-tuple-element.94), channel_id=1, source_target_pairs={{0,1},{1,2},{2,3},{3,4},{4,5},{5,6},{6,7},{7,8},{8,9},{9,10},{10,1... | collective-permute-start | bytes 3538952 | tf_op jit(solution)/shard_map/ppermute | solution.py:167
  77.9 45.0 %collective-permute-start.11 = (f32[256,1152]{1,0:T(8,128)S(1)}, f32[256,1152]{1,0:T(8,128)S(1)}, u32[]{:S(2)}, u32[]{:S(2)}) collective-permute-start(f32[256,1152]{1,0:T(8,128)S(1)} %get-tuple-element.99), channel_id=1, source_target_pairs={{0,1},{1,2},{2,3},{3,4},{4,5},{5,6},{6,7},{7,8},{8,9},{9,10},{10,1... | collective-permute-start | bytes 3538952 | tf_op jit(solution)/shard_map/ppermute | solution.py:167
  80.3 24.1 %collective-permute-start.9 = (f32[128,1152]{1,0:T(8,128)S(1)}, f32[128,1152]{1,0:T(8,128)S(1)}, u32[]{:S(2)}, u32[]{:S(2)}) collective-permute-start(f32[128,1152]{1,0:T(8,128)S(1)} %collective-permute-done.4), channel_id=1, source_target_pairs={{0,112},{16,0},{32,16},{48,32},{64,48},{80,64},{96,80},{112,96},{1... | collective-permute-start | bytes 1769480 | tf_op jit(solution)/shard_map/ppermute | solution.py:181
  92.3 24.7 %collective-permute-start.8 = (f32[128,1152]{1,0:T(8,128)S(1)}, f32[128,1152]{1,0:T(8,128)S(1)}, u32[]{:S(2)}, u32[]{:S(2)}) collective-permute-start(f32[128,1152]{1,0:T(8,128)S(1)} %collective-permute-done.5), channel_id=1, source_target_pairs={{0,112},{16,0},{32,16},{48,32},{64,48},{80,64},{96,80},{112,96},{1... | collective-permute-start | bytes 1769480 | tf_op jit(solution)/shard_map/ppermute | solution.py:181

commit v2 on v1

--- a/solution.py
+++ b/solution.py
@@ -8,6 +8,7 @@
 from jax.sharding import PartitionSpec as P
 
 OWN, AHEAD, FIRST, LAST, NEXT, REST_TEXT, REST_IMAGE = 3, 1, 1, 2, 3, 1, 40
+STRAIGHT = 128
 TILE = 256
 F32, BF16 = jnp.float32, jnp.bfloat16
 ROW_ROW = (((1,), (1,)), ((), ()))
@@ -49,12 +50,15 @@
     low[...], high[...] = value[:cut], value[cut:]
 
 
-def own_kernel(scale_ref, bias_ref, images, texts, partner, image_grad, text_grad, ih, il, th, tl):
-    scale, bias = scale_ref[0], bias_ref[0]
+def split_kernel(scale_ref, bias_ref, images, texts, ih, il, th, tl):
     split_rows(texts, th, tl)
     split_rows(images, ih, il)
+
+
+def own_kernel(scale_ref, bias_ref, ih, il, th, tl, partner, image_grad, text_grad):
+    scale, bias = scale_ref[0], bias_ref[0]
     text = (th[...], tl[...])
-    for k in range(images.shape[0] // TILE):
+    for k in range(ih.shape[0] // TILE):
         rows = pl.ds(k * TILE, TILE)
         image = (ih[rows, :], il[rows, :])
         w = weights(image, text, scale, bias)
@@ -114,18 +118,20 @@
     store_halves(total, refs[-2], refs[-1])
 
 
-def rest_image_kernel(scale_ref, bias_ref, grad_in, uh, ul, nh, nl, back0, back1, out, held0, held1, done0, done1, sems):
+def rest_image_kernel(scale_ref, bias_ref, grad_in, uh, ul, nh, nl, back0, out, held0, middle, held1, done, sem):
     cut, size = back0.shape[0], grad_in.shape[0] // 2
-    copies = []
-    for k, (back, held, done) in enumerate(((back0, held0, done0), (back1, held1, done1))):
-        rows = pl.ds(k * size, size)
-        total = grad_in[rows, :] + mm((uh[rows, :], ul[rows, :]), (nh[...], nl[...]), ROW_COL)
-        done[...] = total[:cut] + back[...]
-        copies.append(pltpu.make_async_copy(done, out.at[pl.ds(k * size, cut), :], sems.at[k]))
-        copies[-1].start()
-        held[...] = total[cut:]
-    for copy in copies:
-        copy.wait()
+
+    def rows_of(start):
+        rows = pl.ds(start, size)
+        return grad_in[rows, :] + mm((uh[rows, :], ul[rows, :]), (nh[...], nl[...]), ROW_COL)
+
+    total = rows_of(0)
+    done[...] = total[:cut] + back0[...]
+    copy = pltpu.make_async_copy(done, out.at[pl.ds(0, cut), :], sem)
+    copy.start()
+    held0[...] = total[cut:]
+    store_halves(rows_of(size), middle, held1)
+    copy.wait()
 
 
 def place_kernel(start, held, back, *refs):
@@ -189,7 +195,8 @@
     rows, width = images.shape
     size = rows // 2
     block, half, piece = ((rows, width), F32), ((rows, width), BF16), ((size, width), F32)
-    quarter = ((size // 2, width), F32)
+    cut = size * STRAIGHT // 256
+    straight, across = ((cut, width), F32), ((size - cut, width), F32)
     ends = [piece, piece]
     low, w_low = ((size, width), BF16), ((size, rows), BF16)
     work = 6 * rows * rows * width
@@ -197,14 +204,13 @@
     last, images, texts = tied(last, images, texts)
     other = crossed(last, -1, False)
     text_next = shifted(texts, "inner", -1)
+    ih, il, th, tl = call(split_kernel, [half] * 4, [scale, bias, images, texts], {}, 0)
+    images, ih = tied(images, ih)
     first = shifted(images[:size], "outer", 1)
-    image_grad, text_grad, ih, il, th, tl = call(
-        own_kernel,
-        [block, block, half, half, half, half],
-        [scale, bias, images, texts, partner.reshape(rows, 1)],
-        {},
-        OWN * work,
-    )
+    image_grad, text_grad = call(
+        own_kernel, [block, block], [scale, bias, ih, il, th, tl, partner.reshape(rows, 1)], {}, OWN * work
+    )
+    image_grad, th = tied(image_grad, th)
     other, th = tied(other, th)
     outer = lax.axis_size("outer") // 2
     last = jnp.where(lax.axis_index("outer") % outer == outer - 1, other, last)
@@ -214,7 +220,7 @@
     )
     straight0, across0, vh, vl, nh, nl = call(
         first_kernel,
-        [quarter, quarter, w_low, w_low, half, half],
+        [straight, across, w_low, w_low, half, half],
         [scale, bias, *kept0, text_next, total],
         {},
         FIRST * work,
@@ -224,7 +230,7 @@
     mine0, next0 = [*kept0, wh, wl], [*kept0, vh, vl]
     straight1, across1, *kept1 = call(
         last_kernel,
-        [quarter, quarter, low, low, w_low, w_low, w_low, w_low],
+        [straight, across, low, low, w_low, w_low, w_low, w_low],
         [scale, bias, last, th, tl, nh, nl],
         {},
         LAST * work,
@@ -240,23 +246,25 @@
         NEXT * work,
     )
     early, late = shifted(early, "inner", 1), shifted(late, "inner", 1)
-    uh, text_grad, across0 = tied(uh, text_grad, across0)
+    uh, text_grad, across0, straight0 = tied(uh, text_grad, across0, straight0)
     across0 = turned(across0, -1)
     text0, text1 = call(rest_text_kernel, ends, [scale, bias, text_grad, *mine0, *mine1], {}, REST_TEXT * work)
-    text0, uh, across1, straight0, straight1 = tied(text0, uh, across1, straight0, straight1)
+    text0, uh, across1 = tied(text0, uh, across1)
     across1 = turned(across1, -1)
-    image_grad, image0, image1 = call(
+    image_grad, image0, middle, image1 = call(
         rest_image_kernel,
-        [block, quarter, quarter],
-        [scale, bias, image_grad, uh, ul, nh, nl, straight0, straight1],
+        [block, across, straight, across],
+        [scale, bias, image_grad, uh, ul, nh, nl, straight0],
         {},
         REST_IMAGE * work,
-        [pltpu.VMEM((size // 2, width), F32)] * 2 + [pltpu.SemaphoreType.DMA((2,))],
+        [pltpu.VMEM((cut, width), F32), pltpu.SemaphoreType.DMA],
         1,
     )
+    image_grad = place(middle, straight1, size, image_grad, images.shape)
+    image_grad = place(image0, across0, cut, image_grad, images.shape)
     text_grad = place(text0, early, 0, None, images.shape)
-    image_grad = place(image0, across0, size // 2, image_grad, images.shape)
-    image_grad = place(image1, across1, size + size // 2, image_grad, images.shape)
+    image_grad, text_grad = tied(image_grad, text_grad)
+    image_grad = place(image1, across1, size + cut, image_grad, images.shape)
     image_grad, late = tied(image_grad, late)
     text_grad = place(text1, late, size, text_grad, images.shape)
     return image_grad, text_grad

time: 126 us -> 124 us (0.984)
  waiting for transfers between devices: 65 us -> 52.7 us
  local copies, waits for them, and re-layouts: 5.42 us -> 13.3 us
  starting transfers between devices: 13.2 us -> 15.6 us
    ppermute x3, waiting for transfers between devices: 8.3 us -> 0.41 us  [crossed(): return lax.ppermute(array, 'outer', pairs)]
    unnamed x6 -> x30, local copies, waits for them, and re-layouts: 1.67 us -> 9.42 us
    ppermute x3, waiting for transfers between devices: 20.8 us -> 13.3 us  [turned(): return lax.ppermute(array, 'outer', pairs)]
    ppermute x6, waiting for transfers between devices: 35.9 us -> 38.9 us  [shifted(): lax.ppermute(array, axis, [(i, (i + by) % size) for i in range(size)])]
    ppermute x3, starting transfers between devices: 0.35 us -> 3.06 us  [turned(): return lax.ppermute(array, 'outer', pairs)]
    pallas_call x7 -> x8, Pallas kernels: 34 us -> 32.1 us  [call(): pl.pallas_call(kernel, out_shape=[jax.ShapeDtypeStruct(s, d) for s, d in...]
    pallas_call x4 -> x5, Pallas kernels: 4.05 us -> 4.93 us  [place(): pl.pallas_call(functools.partial(place_kernel, start), out_shape=jax.Shap...]
  transfers between devices with their start and end apart: 12 -> 12, of which waited for: 7 -> 8; matrix products, arithmetic and copies ran while one was open for 2% -> 2% of each run, Pallas kernels for 28% -> 29%
where the time goes in v2:
time: 124 us; the launch traced here: 122 us
  waiting for transfers between devices  52.7 us (42%)
  Pallas kernels  37 us (30%)
  starting transfers between devices  15.6 us (13%)
  local copies, waits for them, and re-layouts  13.3 us (11%)
  between operations  2.36 us (2%)
  other arithmetic  1.6 us (1%)
    ppermute x6, waiting for transfers between devices, shifted(): lax.ppermute(array, axis, [(i, (i + by) % size) for i in range(size)])  38.9 us
    pallas_call x8, Pallas kernels, call(): pl.pallas_call(kernel, out_shape=[jax.ShapeDtypeStruct(s, d) for s, d in...  32.1 us
    ppermute x3, waiting for transfers between devices, turned(): return lax.ppermute(array, 'outer', pairs)  13.3 us
    unnamed x30, local copies, waits for them, and re-layouts  9.42 us
    ppermute x6, starting transfers between devices, shifted(): lax.ppermute(array, axis, [(i, (i + by) % size) for i in range(size)])  7.72 us
    pallas_call x5, Pallas kernels, place(): pl.pallas_call(functools.partial(place_kernel, start), out_shape=jax.Shap...  4.93 us
    ppermute x3, starting transfers between devices, crossed(): return lax.ppermute(array, 'outer', pairs)  4.79 us
    ppermute x3, starting transfers between devices, turned(): return lax.ppermute(array, 'outer', pairs)  3.06 us
  transfers between devices with their start and end apart: 12, of which 8 were waited for; matrix products, arithmetic and copies ran while one was open for 2% of the time, Pallas kernels for 29%

profile of v2, /device:TPU:224, one launch (start us, length us, event | category | flops | bytes accessed | tf_op | source)
XLA Modules:
  0.0 122.5 jit_solution(6496907243279041661)
XLA Ops:
  0.6 2.5 %slice.6 = f32[256,1152]{1,0:T(8,128)} slice(f32[512,1152]{1,0:T(8,128)} %images), slice={[256:512], [0:1152]} | slice | bytes 2359296 | tf_op jit(solution)/shard_map/slice | solution.py:203
  3.2 3.4 %collective-permute-start.1 = (f32[256,1152]{1,0:T(8,128)}, f32[256,1152]{1,0:T(8,128)}, u32[]{:S(2)}, u32[]{:S(2)}) collective-permute-start(f32[256,1152]{1,0:T(8,128)} %slice.6), channel_id=1, source_target_pairs={{112,240},{240,112},{113,241},{241,113},{114,242},{242,114},{115,2... | collective-permute-start | bytes 3538952 | tf_op jit(solution)/shard_map/ppermute | solution.py:181
  6.5 4.4 %collective-permute-start.2 = (f32[512,1152]{1,0:T(8,128)}, f32[512,1152]{1,0:T(8,128)S(1)}, u32[]{:S(2)}, u32[]{:S(2)}) collective-permute-start(f32[512,1152]{1,0:T(8,128)} %texts), channel_id=1, source_target_pairs={{0,15},{1,0},{2,1},{3,2},{4,3},{5,4},{6,5},{7,6},{8,7},{9,8},{10,9... | collective-permute-start | bytes 7077896 | tf_op jit(solution)/shard_map/ppermute | solution.py:173
  12.3 1.7 %copy-done.1 = f32[512,1152]{1,0:T(8,128)S(1)} copy-done((f32[512,1152]{1,0:T(8,128)S(1)}, f32[512,1152]{1,0:T(8,128)}, u32[]{:S(2)}) %copy-start.1) | copy-done | bytes 2359320
  14.8 1.0 copy-done.8
  15.8 1.0 copy-done.11
  16.9 1.2 slice.7
  18.8 1.3 %copy-done.3 = bf16[512,1152]{1,0:T(8,128)(2,1)S(1)} copy-done((bf16[512,1152]{1,0:T(8,128)(2,1)S(1)}, bf16[512,1152]{1,0:T(8,128)(2,1)}, u32[]{:S(2)}) %copy-start.3) | copy-done | bytes 1179672
  20.1 1.3 %copy-done.6 = bf16[512,1152]{1,0:T(8,128)(2,1)S(1)} copy-done((bf16[512,1152]{1,0:T(8,128)(2,1)S(1)}, bf16[512,1152]{1,0:T(8,128)(2,1)}, u32[]{:S(2)}) %copy-start.6) | copy-done | bytes 1179672
  21.4 1.3 %copy-done.9 = bf16[512,1152]{1,0:T(8,128)(2,1)S(1)} copy-done((bf16[512,1152]{1,0:T(8,128)(2,1)S(1)}, bf16[512,1152]{1,0:T(8,128)(2,1)}, u32[]{:S(2)}) %copy-start.9) | copy-done | bytes 1179672
  22.6 1.3 %copy-done.12 = bf16[512,1152]{1,0:T(8,128)(2,1)S(1)} copy-done((bf16[512,1152]{1,0:T(8,128)(2,1)S(1)}, bf16[512,1152]{1,0:T(8,128)(2,1)}, u32[]{:S(2)}) %copy-start.12) | copy-done | bytes 1179672
  23.9 8.7 %shard_map.69 = (f32[512,1152]{1,0:T(8,128)S(1)}, f32[512,1152]{1,0:T(8,128)S(1)}) custom-call(f32[1]{0:T(128)S(6)} %copy.16.scale_ref, f32[1]{0:T(128)S(6)} %copy.17.bias_ref, bf16[512,1152]{1,0:T(8,128)(2,1)S(1)} %copy-done.3, bf16[512,1152]{1,0:T(8,128)(2,1)S(1)} %copy-done.6, bf16[512,1152]{1,0:T(8,128)(2,1)S(1)} %copy-done.9, ...), custom_call_target="tpu_custom_call" | custom-call | flops 5435817984 | bytes 1048576 | tf_op jit(solution)/shard_map/pallas_call | solution.py:159
  33.1 1.6 %broadcast_select_fusion = f32[256,1152]{1,0:T(8,128)S(1)} fusion(f32[256,1152]{1,0:T(8,128)} %collective-permute-done.1, f32[256,1152]{1,0:T(8,128)} %slice.6, pred[]{:T(512)S(6)} %eq.5), kind=kLoop, calls=%fused_computation | loop fusion | flops 294912 | bytes 3538945 | tf_op jit(solution)/shard_map/jit(_where)/select_n | solution.py:216
  34.9 12.9 %collective-permute-done.piece = f32[256,1152]{1,0:T(8,128)} collective-permute-done((f32[256,1152]{1,0:T(8,128)}, f32[256,1152]{1,0:T(8,128)}, u32[]{:S(2)}, u32[]{:S(2)}) %collective-permute-start) | collective-permute-done | bytes 1179680 | tf_op jit(solution)/shard_map/ppermute | solution.py:173
  47.9 3.6 %shard_map.70 = (bf16[256,1152]{1,0:T(8,128)(2,1)S(1)}, bf16[256,1152]{1,0:T(8,128)(2,1)S(1)}, bf16[256,512]{1,0:T(8,128)(2,1)S(1)}, bf16[256,512]{1,0:T(8,128)(2,1)S(1)}, f32[256,1152]{1,0:T(8,128)S(1)}) custom-call(f32[1]{0:T(128)S(6)} %copy.16.scale_ref, f32[1]{0:T(128)S(6)} %copy.17.bias_ref, f32[256,1152]{1,0:T(8,128)} %collective-permute-done.piece, ...), custom_call_target="tpu_custom_call" | custom-call | flops 1811939328 | bytes 1048576 | tf_op jit(solution)/shard_map/pallas_call | solution.py:159
  51.5 5.8 %collective-permute-done.2.text_next = f32[512,1152]{1,0:T(8,128)S(1)} collective-permute-done((f32[512,1152]{1,0:T(8,128)}, f32[512,1152]{1,0:T(8,128)S(1)}, u32[]{:S(2)}, u32[]{:S(2)}) %collective-permute-start.2) | collective-permute-done | bytes 2359328 | tf_op jit(solution)/shard_map/ppermute | solution.py:173
  57.3 2.8 %shard_map.71 = (f32[128,1152]{1,0:T(8,128)S(1)}, f32[128,1152]{1,0:T(8,128)S(1)}, bf16[256,512]{1,0:T(8,128)(2,1)S(1)}, bf16[256,512]{1,0:T(8,128)(2,1)S(1)}, b...) custom-call(f32[1]{0:T(128)S(6)} %copy.16.scale_ref, f32[1]{0:T(128)S(6)} %copy.17.bias_ref, ...), custom_call_target="tpu_custom_call" | custom-call | flops 1811939328 | bytes 1048576 | tf_op jit(solution)/shard_map/pallas_call | solution.py:159
  60.9 7.3 %collective-permute-done.3.piece = f32[256,1152]{1,0:T(8,128)S(1)} collective-permute-done((f32[256,1152]{1,0:T(8,128)S(1)}, f32[256,1152]{1,0:T(8,128)S(1)}, u32[]{:S(2)}, u32[]{:S(2)}) %collective-permute-start.3) | collective-permute-done | bytes 1179680 | tf_op jit(solution)/shard_map/ppermute | solution.py:187
  68.2 4.6 %shard_map.72 = (f32[128,1152]{1,0:T(8,128)S(1)}, f32[128,1152]{1,0:T(8,128)S(1)}, bf16[256,1152]{1,0:T(8,128)(2,1)S(1)}, bf16[256,1152]{1,0:T(8,128)(2,1)S(1)},...) custom-call(f32[1]{0:T(128)S(6)} %copy.16.scale_ref, ...), custom_call_target="tpu_custom_call" | custom-call | flops 3623878656 | bytes 1048576 | tf_op jit(solution)/shard_map/pallas_call | solution.py:159
  73.8 6.5 %shard_map.73 = (f32[256,1152]{1,0:T(8,128)S(1)}, f32[256,1152]{1,0:T(8,128)S(1)}, bf16[512,512]{1,0:T(8,128)(2,1)S(1)}, bf16[512,512]{1,0:T(8,128)(2,1)S(1)}) custom-call(f32[1]{0:T(128)S(6)} %copy.16.scale_ref, f32[1]{0:T(128)S(6)} %copy.17.bias_ref, bf16[512,1152]{1,0:T(8,128)(2,1)S(1)} %copy-done.4, bf16[512,1152]{1,0:T(8,128)(2,1)S(1)} %copy-done.7, ...), custom_call_target="tpu_custom_call" | custom-call | flops 5435817984 | bytes 1048576 | tf_op jit(solution)/shard_map/pallas_call | solution.py:159
  80.4 2.8 %collective-permute-start.11 = (f32[256,1152]{1,0:T(8,128)S(1)}, f32[256,1152]{1,0:T(8,128)S(1)}, u32[]{:S(2)}, u32[]{:S(2)}) collective-permute-start(f32[256,1152]{1,0:T(8,128)S(1)} %get-tuple-element.107), channel_id=1, source_target_pairs={{0,1},{1,2},{2,3},{3,4},{4,5},{5,6},{6,7},{7,8},{8,9},{9,10},{10,1... | collective-permute-start | bytes 3538952 | tf_op jit(solution)/shard_map/ppermute | solution.py:173
  83.7 2.2 %shard_map.74 = (f32[256,1152]{1,0:T(8,128)S(1)}, f32[256,1152]{1,0:T(8,128)S(1)}) custom-call(f32[1]{0:T(128)S(6)} %copy.16.scale_ref, f32[1]{0:T(128)S(6)} %copy.17.bias_ref, f32[512,1152]{1,0:T(8,128)S(1)} %get-tuple-element.86.text_in, bf16[256,1152]{1,0:T(8,128)(2,1)S(1)} %get-tuple-element.70.ph.refs_0_, ...), custom_call_target="tpu_custom_call" | custom-call | flops 1811939328 | bytes 1048576 | tf_op jit(solution)/shard_map/pallas_call | solution.py:159
  86.0 2.3 %collective-permute-start.7 = (f32[128,1152]{1,0:T(8,128)S(1)}, f32[128,1152]{1,0:T(8,128)S(1)}, u32[]{:S(2)}, u32[]{:S(2)}) collective-permute-start(f32[128,1152]{1,0:T(8,128)S(1)} %collective-permute-done.6), channel_id=1, source_target_pairs={{0,112},{16,0},{32,16},{48,32},{64,48},{80,64},{96,80},{112,96},{1... | collective-permute-start | bytes 1769480 | tf_op jit(solution)/shard_map/ppermute | solution.py:187
  88.3 2.8 %shard_map.75 = (f32[512,1152]{1,0:T(8,128)}, f32[128,1152]{1,0:T(8,128)S(1)}, f32[128,1152]{1,0:T(8,128)S(1)}, f32[128,1152]{1,0:T(8,128)S(1)}) custom-call(f32[1]{0:T(128)S(6)} %copy.16.scale_ref, f32[1]{0:T(128)S(6)} %copy.17.bias_ref, f32[512,1152]{1,0:T(8,128)S(1)} %get-tuple-element.65.grad_in, bf16[512,512]{1,0:T(8,128)(2,1)S(1)} %get-tuple-element.94.uh, ...), custom_call_target="tpu_custom_call" | custom-call | flops 72477573120 | bytes 1048576 | tf_op jit(solution)/shard_map/pallas_call | solution.py:159
  91.1 1.2 collective-permute-done.9.back
  93.2 15.3 %collective-permute-done.10.back = f32[256,1152]{1,0:T(8,128)S(1)} collective-permute-done((f32[256,1152]{1,0:T(8,128)S(1)}, f32[256,1152]{1,0:T(8,128)S(1)}, u32[]{:S(2)}, u32[]{:S(2)}) %collective-permute-start.10) | collective-permute-done | bytes 1179680 | tf_op jit(solution)/shard_map/ppermute | solution.py:173
  108.5 1.1 shard_map.78.refs_0_
  109.7 0.9 shard_map.77.refs_0_
  110.6 6.1 %collective-permute-done.7.back = f32[128,1152]{1,0:T(8,128)S(1)} collective-permute-done((f32[128,1152]{1,0:T(8,128)S(1)}, f32[128,1152]{1,0:T(8,128)S(1)}, u32[]{:S(2)}, u32[]{:S(2)}) %collective-permute-start.7) | collective-permute-done | bytes 589856 | tf_op jit(solution)/shard_map/ppermute | solution.py:187
  116.6 0.9 shard_map.79
  117.5 3.6 %collective-permute-done.11.back = f32[256,1152]{1,0:T(8,128)S(1)} collective-permute-done((f32[256,1152]{1,0:T(8,128)S(1)}, f32[256,1152]{1,0:T(8,128)S(1)}, u32[]{:S(2)}, u32[]{:S(2)}) %collective-permute-start.11) | collective-permute-done | bytes 1179680 | tf_op jit(solution)/shard_map/ppermute | solution.py:173
  121.1 1.1 shard_map.80
  (39 shorter events, 5.6 us)
Async XLA Ops:
  0.6 11.6 %copy-start = (f32[512,1152]{1,0:T(8,128)S(1)}, f32[512,1152]{1,0:T(8,128)}, u32[]{:S(2)}) copy-start(f32[512,1152]{1,0:T(8,128)} %images) | copy-start | bytes 7077892
  3.2 29.9 %collective-permute-start.1 = (f32[256,1152]{1,0:T(8,128)}, f32[256,1152]{1,0:T(8,128)}, u32[]{:S(2)}, u32[]{:S(2)}) collective-permute-start(f32[256,1152]{1,0:T(8,128)} %slice.6), channel_id=1, source_target_pairs={{112,240},{240,112},{113,241},{241,113},{114,242},{242,114},{115,2... | collective-permute-start | bytes 3538952 | tf_op jit(solution)/shard_map/ppermute | solution.py:181
  6.5 50.8 %collective-permute-start.2 = (f32[512,1152]{1,0:T(8,128)}, f32[512,1152]{1,0:T(8,128)S(1)}, u32[]{:S(2)}, u32[]{:S(2)}) collective-permute-start(f32[512,1152]{1,0:T(8,128)} %texts), channel_id=1, source_target_pairs={{0,15},{1,0},{2,1},{3,2},{4,3},{5,4},{6,5},{7,6},{8,7},{9,8},{10,9... | collective-permute-start | bytes 7077896 | tf_op jit(solution)/shard_map/ppermute | solution.py:173
  12.3 1.7 %copy-start.1 = (f32[512,1152]{1,0:T(8,128)S(1)}, f32[512,1152]{1,0:T(8,128)}, u32[]{:S(2)}) copy-start(f32[512,1152]{1,0:T(8,128)} %texts) | copy-start | bytes 7077892
  14.8 1.0 copy-start.8
  15.8 1.0 copy-start.11
  16.9 1.4 %copy-start.2 = (bf16[512,1152]{1,0:T(8,128)(2,1)}, bf16[512,1152]{1,0:T(8,128)(2,1)S(1)}, u32[]{:S(2)}) copy-start(bf16[512,1152]{1,0:T(8,128)(2,1)S(1)} %get-tuple-element.60.ih) | copy-start | bytes 3538948
  16.9 1.8 %copy-start.5 = (bf16[512,1152]{1,0:T(8,128)(2,1)}, bf16[512,1152]{1,0:T(8,128)(2,1)S(1)}, u32[]{:S(2)}) copy-start(bf16[512,1152]{1,0:T(8,128)(2,1)S(1)} %get-tuple-element.61.il) | copy-start | bytes 3538948
  16.9 1.8 %copy-start.14 = (s32[1,512]{1,0:T(1,128)S(1)}, s32[1,512]{1,0:T(1,128)}, u32[]{:S(2)}) copy-start(s32[1,512]{1,0:T(1,128)} %param.7) | copy-start | bytes 6148
  18.7 29.2 %collective-permute-start = (f32[256,1152]{1,0:T(8,128)}, f32[256,1152]{1,0:T(8,128)}, u32[]{:S(2)}, u32[]{:S(2)}) collective-permute-start(f32[256,1152]{1,0:T(8,128)} %slice.7), channel_id=1, source_target_pairs={{0,16},{16,32},{32,48},{48,64},{64,80},{80,96},{96,112},{112,128},... | collective-permute-start | bytes 3538952 | tf_op jit(solution)/shard_map/ppermute | solution.py:173
  18.8 1.3 %copy-start.3 = (bf16[512,1152]{1,0:T(8,128)(2,1)S(1)}, bf16[512,1152]{1,0:T(8,128)(2,1)}, u32[]{:S(2)}) copy-start(bf16[512,1152]{1,0:T(8,128)(2,1)} %copy-done.2) | copy-start | bytes 3538948
  20.1 1.3 %copy-start.6 = (bf16[512,1152]{1,0:T(8,128)(2,1)S(1)}, bf16[512,1152]{1,0:T(8,128)(2,1)}, u32[]{:S(2)}) copy-start(bf16[512,1152]{1,0:T(8,128)(2,1)} %copy-done.5) | copy-start | bytes 3538948
  21.4 1.3 %copy-start.9 = (bf16[512,1152]{1,0:T(8,128)(2,1)S(1)}, bf16[512,1152]{1,0:T(8,128)(2,1)}, u32[]{:S(2)}) copy-start(bf16[512,1152]{1,0:T(8,128)(2,1)} %copy-done.8) | copy-start | bytes 3538948
  22.6 1.3 %copy-start.12 = (bf16[512,1152]{1,0:T(8,128)(2,1)S(1)}, bf16[512,1152]{1,0:T(8,128)(2,1)}, u32[]{:S(2)}) copy-start(bf16[512,1152]{1,0:T(8,128)(2,1)} %copy-done.11) | copy-start | bytes 3538948
  32.6 15.2 %copy-start.10 = (bf16[512,1152]{1,0:T(8,128)(2,1)S(1)}, bf16[512,1152]{1,0:T(8,128)(2,1)}, u32[]{:S(2)}) copy-start(bf16[512,1152]{1,0:T(8,128)(2,1)} %copy-done.8) | copy-start | bytes 3538948
  32.6 15.2 %copy-start.13 = (bf16[512,1152]{1,0:T(8,128)(2,1)S(1)}, bf16[512,1152]{1,0:T(8,128)(2,1)}, u32[]{:S(2)}) copy-start(bf16[512,1152]{1,0:T(8,128)(2,1)} %copy-done.11) | copy-start | bytes 3538948
  34.7 33.5 %collective-permute-start.3 = (f32[256,1152]{1,0:T(8,128)S(1)}, f32[256,1152]{1,0:T(8,128)S(1)}, u32[]{:S(2)}, u32[]{:S(2)}) collective-permute-start(f32[256,1152]{1,0:T(8,128)S(1)} %broadcast_select_fusion), channel_id=1, source_target_pairs={{0,16},{16,32},{32,48},{48,64},{64,80},{80,96},{96,112},{112,0},{1... | collective-permute-start | bytes 3538952 | tf_op jit(solution)/shard_map/ppermute | solution.py:187
  60.1 20.2 %collective-permute-start.4 = (f32[128,1152]{1,0:T(8,128)S(1)}, f32[128,1152]{1,0:T(8,128)S(1)}, u32[]{:S(2)}, u32[]{:S(2)}) collective-permute-start(f32[128,1152]{1,0:T(8,128)S(1)} %get-tuple-element.84), channel_id=1, source_target_pairs={{0,128},{128,0},{16,16},{32,32},{48,48},{64,64},{80,80},{96,96},{1... | collective-permute-start | bytes 1769480 | tf_op jit(solution)/shard_map/ppermute | solution.py:181
  60.9 22.4 %collective-permute-start.5 = (f32[128,1152]{1,0:T(8,128)S(1)}, f32[128,1152]{1,0:T(8,128)S(1)}, u32[]{:S(2)}, u32[]{:S(2)}) collective-permute-start(f32[128,1152]{1,0:T(8,128)S(1)} %get-tuple-element.85), channel_id=1, source_target_pairs={{0,240},{16,0},{32,16},{48,32},{64,48},{80,64},{96,80},{112,96},{1... | collective-permute-start | bytes 1769480 | tf_op jit(solution)/shard_map/ppermute | solution.py:173
  68.2 5.6 %copy-start.4 = (bf16[512,1152]{1,0:T(8,128)(2,1)S(1)}, bf16[512,1152]{1,0:T(8,128)(2,1)}, u32[]{:S(2)}) copy-start(bf16[512,1152]{1,0:T(8,128)(2,1)} %copy-done.2) | copy-start | bytes 3538948
  68.2 5.6 %copy-start.7 = (bf16[512,1152]{1,0:T(8,128)(2,1)S(1)}, bf16[512,1152]{1,0:T(8,128)(2,1)}, u32[]{:S(2)}) copy-start(bf16[512,1152]{1,0:T(8,128)(2,1)} %copy-done.5) | copy-start | bytes 3538948
  72.8 13.2 %collective-permute-start.6 = (f32[128,1152]{1,0:T(8,128)S(1)}, f32[128,1152]{1,0:T(8,128)S(1)}, u32[]{:S(2)}, u32[]{:S(2)}) collective-permute-start(f32[128,1152]{1,0:T(8,128)S(1)} %get-tuple-element.93), channel_id=1, source_target_pairs={{0,128},{128,0},{16,16},{32,32},{48,48},{64,64},{80,80},{96,96},{1... | collective-permute-start | bytes 1769480 | tf_op jit(solution)/shard_map/ppermute | solution.py:181
  73.5 18.8 %collective-permute-start.9 = (f32[128,1152]{1,0:T(8,128)S(1)}, f32[128,1152]{1,0:T(8,128)S(1)}, u32[]{:S(2)}, u32[]{:S(2)}) collective-permute-start(f32[128,1152]{1,0:T(8,128)S(1)} %get-tuple-element.102), channel_id=1, source_target_pairs={{0,240},{16,0},{32,16},{48,32},{64,48},{80,64},{96,80},{112,96},{1... | collective-permute-start | bytes 1769480 | tf_op jit(solution)/shard_map/ppermute | solution.py:173
  80.3 28.2 %collective-permute-start.10 = (f32[256,1152]{1,0:T(8,128)S(1)}, f32[256,1152]{1,0:T(8,128)S(1)}, u32[]{:S(2)}, u32[]{:S(2)}) collective-permute-start(f32[256,1152]{1,0:T(8,128)S(1)} %get-tuple-element.105), channel_id=1, source_target_pairs={{0,1},{1,2},{2,3},{3,4},{4,5},{5,6},{6,7},{7,8},{8,9},{9,10},{10,1... | collective-permute-start | bytes 3538952 | tf_op jit(solution)/shard_map/ppermute | solution.py:173
  80.4 40.8 %collective-permute-start.11 = (f32[256,1152]{1,0:T(8,128)S(1)}, f32[256,1152]{1,0:T(8,128)S(1)}, u32[]{:S(2)}, u32[]{:S(2)}) collective-permute-start(f32[256,1152]{1,0:T(8,128)S(1)} %get-tuple-element.107), channel_id=1, source_target_pairs={{0,1},{1,2},{2,3},{3,4},{4,5},{5,6},{6,7},{7,8},{8,9},{9,10},{10,1... | collective-permute-start | bytes 3538952 | tf_op jit(solution)/shard_map/ppermute | solution.py:173
  83.2 26.4 %collective-permute-start.8 = (f32[128,1152]{1,0:T(8,128)S(1)}, f32[128,1152]{1,0:T(8,128)S(1)}, u32[]{:S(2)}, u32[]{:S(2)}) collective-permute-start(f32[128,1152]{1,0:T(8,128)S(1)} %collective-permute-done.4), channel_id=1, source_target_pairs={{0,112},{16,0},{32,16},{48,32},{64,48},{80,64},{96,80},{112,96},{1... | collective-permute-start | bytes 1769480 | tf_op jit(solution)/shard_map/ppermute | solution.py:187
  86.0 30.6 %collective-permute-start.7 = (f32[128,1152]{1,0:T(8,128)S(1)}, f32[128,1152]{1,0:T(8,128)S(1)}, u32[]{:S(2)}, u32[]{:S(2)}) collective-permute-start(f32[128,1152]{1,0:T(8,128)S(1)} %collective-permute-done.6), channel_id=1, source_target_pairs={{0,112},{16,0},{32,16},{48,32},{64,48},{80,64},{96,80},{112,96},{1... | collective-permute-start | bytes 1769480 | tf_op jit(solution)/shard_map/ppermute | solution.py:187

commit v3 on v2

--- a/solution.py
+++ b/solution.py
@@ -173,12 +173,27 @@
     return lax.ppermute(array, axis, [(i, (i + by) % size) for i in range(size)])
 
 
-def crossed(array, at, keep=True):
+def crossed(array, at):
     half = lax.axis_size("outer") // 2
-    pairs = [(i, (i + half) % (2 * half)) for i in range(2 * half) if i % half == at % half]
-    if keep:
-        pairs += [(i, i) for i in range(2 * half) if i % half != at % half]
+    pairs = [(i, (i + half) % (2 * half) if i % half == at % half else i) for i in range(2 * half)]
     return lax.ppermute(array, "outer", pairs)
+
+
+def exchanged(array):
+    half, inner = lax.axis_size("outer") // 2, lax.axis_size("inner")
+    ends = ((half - 1, 2 * half - 1), (2 * half - 1, half - 1))
+    pairs = [(a * inner + i, b * inner + i) for a, b in ends for i in range(0, inner, 2)]
+    return lax.ppermute(array, ("outer", "inner"), pairs)
+
+
+def advanced(array):
+    half, inner = lax.axis_size("outer") // 2, lax.axis_size("inner")
+    pairs = []
+    for o in range(2 * half):
+        for i in range(inner):
+            to = (o + 1) % (2 * half) if i % 2 else o // half * half + (o + 1) % half
+            pairs.append((o * inner + i, to * inner + i))
+    return lax.ppermute(array, ("outer", "inner"), pairs)
 
 
 def turned(array, by):
@@ -200,21 +215,22 @@
     ends = [piece, piece]
     low, w_low = ((size, width), BF16), ((size, rows), BF16)
     work = 6 * rows * rows * width
-    last = images[size:]
-    last, images, texts = tied(last, images, texts)
-    other = crossed(last, -1, False)
     text_next = shifted(texts, "inner", -1)
+    other = exchanged(images)
     ih, il, th, tl = call(split_kernel, [half] * 4, [scale, bias, images, texts], {}, 0)
-    images, ih = tied(images, ih)
-    first = shifted(images[:size], "outer", 1)
+    other, images, ih = tied(other, images, ih)
+    half_outer = lax.axis_size("outer") // 2
+    edge = lax.axis_index("outer") % half_outer == half_outer - 1
+    take = jnp.logical_and(edge, lax.axis_index("inner") % 2 == 0)
+    first = jnp.where(take, other[:size], images[:size])
+    first, images, other = tied(first, images, other)
+    last = jnp.where(take, other[size:], images[size:])
+    last, ih = tied(last, ih)
+    first, last = advanced(first), advanced(last)
     image_grad, text_grad = call(
         own_kernel, [block, block], [scale, bias, ih, il, th, tl, partner.reshape(rows, 1)], {}, OWN * work
     )
     image_grad, th = tied(image_grad, th)
-    other, th = tied(other, th)
-    outer = lax.axis_size("outer") // 2
-    last = jnp.where(lax.axis_index("outer") % outer == outer - 1, other, last)
-    last = turned(last, 1)
     *kept0, wh, wl, total = call(
         ahead_kernel, [low, low, w_low, w_low, piece], [scale, bias, first, th, tl], {}, AHEAD * work
     )

time: 124 us -> 123 us (level)
  local copies, waits for them, and re-layouts: 13.3 us -> 9.59 us
  other arithmetic: 1.6 us -> 4.95 us
  waiting for transfers between devices: 52.7 us -> 51 us
  Pallas kernels: 37 us -> 38.5 us
    ppermute x6 -> x5, waiting for transfers between devices: 38.9 us -> 4.45 us  [shifted(): lax.ppermute(array, axis, [(i, (i + by) % size) for i in range(size)])]
    ppermute x0 -> x3, waiting for transfers between devices: none -> 27.4 us  [the longest x1 17.5 us: exchanged(): return lax.ppermute(array, ('outer', 'inner'), pairs)]
    ppermute x3 -> x2, waiting for transfers between devices: 13.3 us -> 19.1 us  [turned(): return lax.ppermute(array, 'outer', pairs)]
    slice x2 -> x0, local copies, waits for them, and re-layouts: 3.7 us -> none  [the longest x1 2.51 us: shards(): last = images[size:]]
    ppermute x0 -> x3, starting transfers between devices: none -> 3.49 us  [the longest x1 3.4 us: exchanged(): return lax.ppermute(array, ('outer', 'inner'), pairs)]
    ppermute x3 -> x2, starting transfers between devices: 4.79 us -> 1.4 us  [crossed(): return lax.ppermute(array, 'outer', pairs)]
    select_n x1 -> x2, other arithmetic: 1.6 us -> 4.95 us  [the longest x1 2.52 us: shards(): first = jnp.where(take, other[:size], images[:size])]
    pallas_call x8, Pallas kernels: 32.1 us -> 33.5 us  [call(): pl.pallas_call(kernel, out_shape=[jax.ShapeDtypeStruct(s, d) for s, d in...]
  transfers between devices with their start and end apart: 12 -> 12, of which waited for: 8 -> 8; matrix products, arithmetic and copies ran while one was open for 2% -> 4% of each run, Pallas kernels for 29% -> 31%
where the time goes in v3:
time: 123 us; the launch traced here: 121 us
  waiting for transfers between devices  51 us (41%)
  Pallas kernels  38.5 us (31%)
  starting transfers between devices  15 us (12%)
  local copies, waits for them, and re-layouts  9.59 us (8%)
  other arithmetic  4.95 us (4%)
  between operations  2.36 us (2%)
    pallas_call x8, Pallas kernels, call(): pl.pallas_call(kernel, out_shape=[jax.ShapeDtypeStruct(s, d) for s, d in...  33.5 us
    ppermute x2, waiting for transfers between devices, turned(): return lax.ppermute(array, 'outer', pairs)  19.1 us
    ppermute x1, waiting for transfers between devices, exchanged(): return lax.ppermute(array, ('outer', 'inner'), pairs)  17.5 us
    ppermute x2, waiting for transfers between devices, advanced(): return lax.ppermute(array, ('outer', 'inner'), pairs)  9.93 us
    unnamed x30, local copies, waits for them, and re-layouts  9.45 us
    ppermute x5, starting transfers between devices, shifted(): lax.ppermute(array, axis, [(i, (i + by) % size) for i in range(size)])  6.89 us
    pallas_call x5, Pallas kernels, place(): pl.pallas_call(functools.partial(place_kernel, start), out_shape=jax.Shap...  4.93 us
    ppermute x5, waiting for transfers between devices, shifted(): lax.ppermute(array, axis, [(i, (i + by) % size) for i in range(size)])  4.45 us
  transfers between devices with their start and end apart: 12, of which 8 were waited for; matrix products, arithmetic and copies ran while one was open for 4% of the time, Pallas kernels for 31%

profile of v3, /device:TPU:224, one launch (start us, length us, event | category | flops | bytes accessed | tf_op | source)
XLA Modules:
  0.0 121.3 jit_solution(9852649589480272486)
XLA Ops:
  0.6 3.4 %collective-permute-start = (f32[512,1152]{1,0:T(8,128)}, f32[512,1152]{1,0:T(8,128)}, u32[]{:S(2)}, u32[]{:S(2)}) collective-permute-start(f32[512,1152]{1,0:T(8,128)} %images.1), channel_id=1, source_target_pairs={{112,240},{114,242},{116,244},{118,246},{120,248},{122,250},{124,2... | collective-permute-start | bytes 7077896 | tf_op jit(solution)/shard_map/ppermute | solution.py:186
  4.0 3.6 %collective-permute-start.2 = (f32[512,1152]{1,0:T(8,128)}, f32[512,1152]{1,0:T(8,128)S(1)}, u32[]{:S(2)}, u32[]{:S(2)}) collective-permute-start(f32[512,1152]{1,0:T(8,128)} %texts.1), channel_id=1, source_target_pairs={{0,15},{1,0},{2,1},{3,2},{4,3},{5,4},{6,5},{7,6},{8,7},{9,8},{10,9... | collective-permute-start | bytes 7077896 | tf_op jit(solution)/shard_map/ppermute | solution.py:173
  8.9 1.7 %copy-done = f32[512,1152]{1,0:T(8,128)S(1)} copy-done((f32[512,1152]{1,0:T(8,128)S(1)}, f32[512,1152]{1,0:T(8,128)}, u32[]{:S(2)}) %copy-start) | copy-done | bytes 2359320
  10.6 1.7 %copy-done.1 = f32[512,1152]{1,0:T(8,128)S(1)} copy-done((f32[512,1152]{1,0:T(8,128)S(1)}, f32[512,1152]{1,0:T(8,128)}, u32[]{:S(2)}) %copy-start.1) | copy-done | bytes 2359320
  13.1 1.0 copy-done.11
  14.2 17.5 %collective-permute-done = f32[512,1152]{1,0:T(8,128)} collective-permute-done((f32[512,1152]{1,0:T(8,128)}, f32[512,1152]{1,0:T(8,128)}, u32[]{:S(2)}, u32[]{:S(2)}) %collective-permute-start) | collective-permute-done | bytes 2359328 | tf_op jit(solution)/shard_map/ppermute | solution.py:186
  31.7 2.5 %slice_select_fusion.1 = f32[256,1152]{1,0:T(8,128)} fusion(f32[512,1152]{1,0:T(8,128)S(1)} %copy-done, f32[512,1152]{1,0:T(8,128)} %collective-permute-done, pred[]{:T(512)S(6)} %and.16), kind=kLoop, calls=%fused_computation.1 | loop fusion | flops 294912 | bytes 3538945 | tf_op jit(solution)/shard_map/jit(_where)/select_n | solution.py:225
  34.3 2.4 %slice_select_fusion = f32[256,1152]{1,0:T(8,128)} fusion(f32[512,1152]{1,0:T(8,128)S(1)} %copy-done, f32[512,1152]{1,0:T(8,128)} %collective-permute-done, pred[]{:T(512)S(6)} %and.16), kind=kLoop, calls=%fused_computation | loop fusion | flops 294912 | bytes 3538945 | tf_op jit(solution)/shard_map/jit(_where)/select_n | solution.py:227
  36.9 1.3 %copy-done.3 = bf16[512,1152]{1,0:T(8,128)(2,1)S(1)} copy-done((bf16[512,1152]{1,0:T(8,128)(2,1)S(1)}, bf16[512,1152]{1,0:T(8,128)(2,1)}, u32[]{:S(2)}) %copy-start.3) | copy-done | bytes 1179672
  38.2 1.3 %copy-done.6 = bf16[512,1152]{1,0:T(8,128)(2,1)S(1)} copy-done((bf16[512,1152]{1,0:T(8,128)(2,1)S(1)}, bf16[512,1152]{1,0:T(8,128)(2,1)}, u32[]{:S(2)}) %copy-start.6) | copy-done | bytes 1179672
  39.5 1.3 %copy-done.9 = bf16[512,1152]{1,0:T(8,128)(2,1)S(1)} copy-done((bf16[512,1152]{1,0:T(8,128)(2,1)S(1)}, bf16[512,1152]{1,0:T(8,128)(2,1)}, u32[]{:S(2)}) %copy-start.9) | copy-done | bytes 1179672
  40.7 1.3 %copy-done.12 = bf16[512,1152]{1,0:T(8,128)(2,1)S(1)} copy-done((bf16[512,1152]{1,0:T(8,128)(2,1)S(1)}, bf16[512,1152]{1,0:T(8,128)(2,1)}, u32[]{:S(2)}) %copy-start.12) | copy-done | bytes 1179672
  42.0 8.7 %shard_map.69 = (f32[512,1152]{1,0:T(8,128)S(1)}, f32[512,1152]{1,0:T(8,128)S(1)}) custom-call(f32[1]{0:T(128)S(6)} %copy.16.scale_ref, f32[1]{0:T(128)S(6)} %copy.17.bias_ref, bf16[512,1152]{1,0:T(8,128)(2,1)S(1)} %copy-done.3, bf16[512,1152]{1,0:T(8,128)(2,1)S(1)} %copy-done.6, bf16[512,1152]{1,0:T(8,128)(2,1)S(1)} %copy-done.9, ...), custom_call_target="tpu_custom_call" | custom-call | flops 5435817984 | bytes 1048576 | tf_op jit(solution)/shard_map/pallas_call | solution.py:159
  50.7 4.8 %collective-permute-done.1.piece = f32[256,1152]{1,0:T(8,128)} collective-permute-done((f32[256,1152]{1,0:T(8,128)}, f32[256,1152]{1,0:T(8,128)}, u32[]{:S(2)}, u32[]{:S(2)}) %collective-permute-start.1) | collective-permute-done | bytes 1179680 | tf_op jit(solution)/shard_map/ppermute | solution.py:196
  55.5 3.6 %shard_map.70 = (bf16[256,1152]{1,0:T(8,128)(2,1)S(1)}, bf16[256,1152]{1,0:T(8,128)(2,1)S(1)}, bf16[256,512]{1,0:T(8,128)(2,1)S(1)}, bf16[256,512]{1,0:T(8,128)(2,1)S(1)}, f32[256,1152]{1,0:T(8,128)S(1)}) custom-call(f32[1]{0:T(128)S(6)} %copy.16.scale_ref, f32[1]{0:T(128)S(6)} %copy.17.bias_ref, f32[256,1152]{1,0:T(8,128)} %collective-permute-done.1.piece, ...), custom_call_target="tpu_custom_call" | custom-call | flops 1811939328 | bytes 1048576 | tf_op jit(solution)/shard_map/pallas_call | solution.py:159
  59.2 2.8 %shard_map.71 = (f32[128,1152]{1,0:T(8,128)S(1)}, f32[128,1152]{1,0:T(8,128)S(1)}, bf16[256,512]{1,0:T(8,128)(2,1)S(1)}, bf16[256,512]{1,0:T(8,128)(2,1)S(1)}, b...) custom-call(f32[1]{0:T(128)S(6)} %copy.16.scale_ref, f32[1]{0:T(128)S(6)} %copy.17.bias_ref, ...), custom_call_target="tpu_custom_call" | custom-call | flops 1811939328 | bytes 1048576 | tf_op jit(solution)/shard_map/pallas_call | solution.py:159
  63.0 5.1 %collective-permute-done.3.piece = f32[256,1152]{1,0:T(8,128)} collective-permute-done((f32[256,1152]{1,0:T(8,128)}, f32[256,1152]{1,0:T(8,128)}, u32[]{:S(2)}, u32[]{:S(2)}) %collective-permute-start.3) | collective-permute-done | bytes 1179680 | tf_op jit(solution)/shard_map/ppermute | solution.py:196
  68.1 6.0 %shard_map.72 = (f32[128,1152]{1,0:T(8,128)S(1)}, f32[128,1152]{1,0:T(8,128)S(1)}, bf16[256,1152]{1,0:T(8,128)(2,1)S(1)}, bf16[256,1152]{1,0:T(8,128)(2,1)S(1)},...) custom-call(f32[1]{0:T(128)S(6)} %copy.16.scale_ref, ...), custom_call_target="tpu_custom_call" | custom-call | flops 3623878656 | bytes 1048576 | tf_op jit(solution)/shard_map/pallas_call | solution.py:159
  74.9 6.5 %shard_map.73 = (f32[256,1152]{1,0:T(8,128)S(1)}, f32[256,1152]{1,0:T(8,128)S(1)}, bf16[512,512]{1,0:T(8,128)(2,1)S(1)}, bf16[512,512]{1,0:T(8,128)(2,1)S(1)}) custom-call(f32[1]{0:T(128)S(6)} %copy.16.scale_ref, f32[1]{0:T(128)S(6)} %copy.17.bias_ref, bf16[512,1152]{1,0:T(8,128)(2,1)S(1)} %copy-done.4, bf16[512,1152]{1,0:T(8,128)(2,1)S(1)} %copy-done.7, ...), custom_call_target="tpu_custom_call" | custom-call | flops 5435817984 | bytes 1048576 | tf_op jit(solution)/shard_map/pallas_call | solution.py:159
  81.5 2.8 %collective-permute-start.11 = (f32[256,1152]{1,0:T(8,128)S(1)}, f32[256,1152]{1,0:T(8,128)S(1)}, u32[]{:S(2)}, u32[]{:S(2)}) collective-permute-start(f32[256,1152]{1,0:T(8,128)S(1)} %get-tuple-element.109), channel_id=1, source_target_pairs={{0,1},{1,2},{2,3},{3,4},{4,5},{5,6},{6,7},{7,8},{8,9},{9,10},{10,1... | collective-permute-start | bytes 3538952 | tf_op jit(solution)/shard_map/ppermute | solution.py:173
  84.4 0.9 collective-permute-start.8
  85.2 2.2 %shard_map.74 = (f32[256,1152]{1,0:T(8,128)S(1)}, f32[256,1152]{1,0:T(8,128)S(1)}) custom-call(f32[1]{0:T(128)S(6)} %copy.16.scale_ref, f32[1]{0:T(128)S(6)} %copy.17.bias_ref, f32[512,1152]{1,0:T(8,128)S(1)} %get-tuple-element.88.text_in, bf16[256,1152]{1,0:T(8,128)(2,1)S(1)} %get-tuple-element.72.ph.refs_0_, ...), custom_call_target="tpu_custom_call" | custom-call | flops 1811939328 | bytes 1048576 | tf_op jit(solution)/shard_map/pallas_call | solution.py:159
  87.5 2.3 %collective-permute-start.7 = (f32[128,1152]{1,0:T(8,128)S(1)}, f32[128,1152]{1,0:T(8,128)S(1)}, u32[]{:S(2)}, u32[]{:S(2)}) collective-permute-start(f32[128,1152]{1,0:T(8,128)S(1)} %collective-permute-done.6), channel_id=1, source_target_pairs={{0,112},{16,0},{32,16},{48,32},{64,48},{80,64},{96,80},{112,96},{1... | collective-permute-start | bytes 1769480 | tf_op jit(solution)/shard_map/ppermute | solution.py:202
  89.8 2.8 %shard_map.75 = (f32[512,1152]{1,0:T(8,128)}, f32[128,1152]{1,0:T(8,128)S(1)}, f32[128,1152]{1,0:T(8,128)S(1)}, f32[128,1152]{1,0:T(8,128)S(1)}) custom-call(f32[1]{0:T(128)S(6)} %copy.16.scale_ref, f32[1]{0:T(128)S(6)} %copy.17.bias_ref, f32[512,1152]{1,0:T(8,128)S(1)} %get-tuple-element.69.grad_in, bf16[512,512]{1,0:T(8,128)(2,1)S(1)} %get-tuple-element.96.uh, ...), custom_call_target="tpu_custom_call" | custom-call | flops 72477573120 | bytes 1048576 | tf_op jit(solution)/shard_map/pallas_call | solution.py:159
  92.6 1.5 %collective-permute-done.9.back = f32[128,1152]{1,0:T(8,128)S(1)} collective-permute-done((f32[128,1152]{1,0:T(8,128)S(1)}, f32[128,1152]{1,0:T(8,128)S(1)}, u32[]{:S(2)}, u32[]{:S(2)}) %collective-permute-start.9) | collective-permute-done | bytes 589856 | tf_op jit(solution)/shard_map/ppermute | solution.py:173
  94.1 0.9 shard_map.76.refs_0_
  95.0 10.8 %collective-permute-done.8.back = f32[128,1152]{1,0:T(8,128)S(1)} collective-permute-done((f32[128,1152]{1,0:T(8,128)S(1)}, f32[128,1152]{1,0:T(8,128)S(1)}, u32[]{:S(2)}, u32[]{:S(2)}) %collective-permute-start.8) | collective-permute-done | bytes 589856 | tf_op jit(solution)/shard_map/ppermute | solution.py:202
  105.8 0.9 shard_map.77.refs_0_
  107.3 1.1 shard_map.78.refs_0_
  108.5 8.3 %collective-permute-done.7.back = f32[128,1152]{1,0:T(8,128)S(1)} collective-permute-done((f32[128,1152]{1,0:T(8,128)S(1)}, f32[128,1152]{1,0:T(8,128)S(1)}, u32[]{:S(2)}, u32[]{:S(2)}) %collective-permute-start.7) | collective-permute-done | bytes 589856 | tf_op jit(solution)/shard_map/ppermute | solution.py:202
  117.6 2.3 %collective-permute-done.11.back = f32[256,1152]{1,0:T(8,128)S(1)} collective-permute-done((f32[256,1152]{1,0:T(8,128)S(1)}, f32[256,1152]{1,0:T(8,128)S(1)}, u32[]{:S(2)}, u32[]{:S(2)}) %collective-permute-start.11) | collective-permute-done | bytes 1179680 | tf_op jit(solution)/shard_map/ppermute | solution.py:173
  120.0 1.1 shard_map.80
  (38 shorter events, 4.5 us)
Async XLA Ops:
  0.6 31.1 %collective-permute-start = (f32[512,1152]{1,0:T(8,128)}, f32[512,1152]{1,0:T(8,128)}, u32[]{:S(2)}, u32[]{:S(2)}) collective-permute-start(f32[512,1152]{1,0:T(8,128)} %images.1), channel_id=1, source_target_pairs={{112,240},{114,242},{116,244},{118,246},{120,248},{122,250},{124,2... | collective-permute-start | bytes 7077896 | tf_op jit(solution)/shard_map/ppermute | solution.py:186
  4.0 55.1 %collective-permute-start.2 = (f32[512,1152]{1,0:T(8,128)}, f32[512,1152]{1,0:T(8,128)S(1)}, u32[]{:S(2)}, u32[]{:S(2)}) collective-permute-start(f32[512,1152]{1,0:T(8,128)} %texts.1), channel_id=1, source_target_pairs={{0,15},{1,0},{2,1},{3,2},{4,3},{5,4},{6,5},{7,6},{8,7},{9,8},{10,9... | collective-permute-start | bytes 7077896 | tf_op jit(solution)/shard_map/ppermute | solution.py:173
  8.9 1.7 %copy-start = (f32[512,1152]{1,0:T(8,128)S(1)}, f32[512,1152]{1,0:T(8,128)}, u32[]{:S(2)}) copy-start(f32[512,1152]{1,0:T(8,128)} %images.1) | copy-start | bytes 7077892
  10.6 1.7 %copy-start.1 = (f32[512,1152]{1,0:T(8,128)S(1)}, f32[512,1152]{1,0:T(8,128)}, u32[]{:S(2)}) copy-start(f32[512,1152]{1,0:T(8,128)} %texts.1) | copy-start | bytes 7077892
  13.1 1.0 copy-start.11
  14.2 20.0 %copy-start.2 = (bf16[512,1152]{1,0:T(8,128)(2,1)}, bf16[512,1152]{1,0:T(8,128)(2,1)S(1)}, u32[]{:S(2)}) copy-start(bf16[512,1152]{1,0:T(8,128)(2,1)S(1)} %get-tuple-element.64.ih) | copy-start | bytes 3538948
  14.2 20.0 %copy-start.5 = (bf16[512,1152]{1,0:T(8,128)(2,1)}, bf16[512,1152]{1,0:T(8,128)(2,1)S(1)}, u32[]{:S(2)}) copy-start(bf16[512,1152]{1,0:T(8,128)(2,1)S(1)} %get-tuple-element.65.il) | copy-start | bytes 3538948
  14.2 20.1 %copy-start.8 = (bf16[512,1152]{1,0:T(8,128)(2,1)}, bf16[512,1152]{1,0:T(8,128)(2,1)S(1)}, u32[]{:S(2)}) copy-start(bf16[512,1152]{1,0:T(8,128)(2,1)S(1)} %get-tuple-element.71.th) | copy-start | bytes 3538948
  34.2 2.5 %copy-start.14 = (s32[1,512]{1,0:T(1,128)S(1)}, s32[1,512]{1,0:T(1,128)}, u32[]{:S(2)}) copy-start(s32[1,512]{1,0:T(1,128)} %param.7) | copy-start | bytes 6148
  34.2 21.3 %collective-permute-start.1 = (f32[256,1152]{1,0:T(8,128)}, f32[256,1152]{1,0:T(8,128)}, u32[]{:S(2)}, u32[]{:S(2)}) collective-permute-start(f32[256,1152]{1,0:T(8,128)} %slice_select_fusion.1), channel_id=1, source_target_pairs={{0,16},{1,17},{2,18},{3,19},{4,20},{5,21},{6,22},{7,23},{8,24},{9,... | collective-permute-start | bytes 3538952 | tf_op jit(solution)/shard_map/ppermute | solution.py:196
  36.8 31.4 %collective-permute-start.3 = (f32[256,1152]{1,0:T(8,128)}, f32[256,1152]{1,0:T(8,128)}, u32[]{:S(2)}, u32[]{:S(2)}) collective-permute-start(f32[256,1152]{1,0:T(8,128)} %slice_select_fusion), channel_id=1, source_target_pairs={{0,16},{1,17},{2,18},{3,19},{4,20},{5,21},{6,22},{7,23},{8,24},{9,... | collective-permute-start | bytes 3538952 | tf_op jit(solution)/shard_map/ppermute | solution.py:196
  36.9 1.3 %copy-start.3 = (bf16[512,1152]{1,0:T(8,128)(2,1)S(1)}, bf16[512,1152]{1,0:T(8,128)(2,1)}, u32[]{:S(2)}) copy-start(bf16[512,1152]{1,0:T(8,128)(2,1)} %copy-done.2) | copy-start | bytes 3538948
  38.2 1.3 %copy-start.6 = (bf16[512,1152]{1,0:T(8,128)(2,1)S(1)}, bf16[512,1152]{1,0:T(8,128)(2,1)}, u32[]{:S(2)}) copy-start(bf16[512,1152]{1,0:T(8,128)(2,1)} %copy-done.5) | copy-start | bytes 3538948
  39.5 1.3 %copy-start.9 = (bf16[512,1152]{1,0:T(8,128)(2,1)S(1)}, bf16[512,1152]{1,0:T(8,128)(2,1)}, u32[]{:S(2)}) copy-start(bf16[512,1152]{1,0:T(8,128)(2,1)} %copy-done.8) | copy-start | bytes 3538948
  40.7 1.3 %copy-start.12 = (bf16[512,1152]{1,0:T(8,128)(2,1)S(1)}, bf16[512,1152]{1,0:T(8,128)(2,1)}, u32[]{:S(2)}) copy-start(bf16[512,1152]{1,0:T(8,128)(2,1)} %copy-done.11) | copy-start | bytes 3538948
  42.0 13.5 %copy-start.10 = (bf16[512,1152]{1,0:T(8,128)(2,1)S(1)}, bf16[512,1152]{1,0:T(8,128)(2,1)}, u32[]{:S(2)}) copy-start(bf16[512,1152]{1,0:T(8,128)(2,1)} %copy-done.8) | copy-start | bytes 3538948
  42.0 13.5 %copy-start.13 = (bf16[512,1152]{1,0:T(8,128)(2,1)S(1)}, bf16[512,1152]{1,0:T(8,128)(2,1)}, u32[]{:S(2)}) copy-start(bf16[512,1152]{1,0:T(8,128)(2,1)} %copy-done.11) | copy-start | bytes 3538948
  62.0 19.5 %collective-permute-start.4 = (f32[128,1152]{1,0:T(8,128)S(1)}, f32[128,1152]{1,0:T(8,128)S(1)}, u32[]{:S(2)}, u32[]{:S(2)}) collective-permute-start(f32[128,1152]{1,0:T(8,128)S(1)} %get-tuple-element.86), channel_id=1, source_target_pairs={{0,128},{16,16},{32,32},{48,48},{64,64},{80,80},{96,96},{112,112},... | collective-permute-start | bytes 1769480 | tf_op jit(solution)/shard_map/ppermute | solution.py:179
  62.7 21.7 %collective-permute-start.5 = (f32[128,1152]{1,0:T(8,128)S(1)}, f32[128,1152]{1,0:T(8,128)S(1)}, u32[]{:S(2)}, u32[]{:S(2)}) collective-permute-start(f32[128,1152]{1,0:T(8,128)S(1)} %get-tuple-element.87), channel_id=1, source_target_pairs={{0,240},{16,0},{32,16},{48,32},{64,48},{80,64},{96,80},{112,96},{1... | collective-permute-start | bytes 1769480 | tf_op jit(solution)/shard_map/ppermute | solution.py:173
  68.1 6.8 %copy-start.4 = (bf16[512,1152]{1,0:T(8,128)(2,1)S(1)}, bf16[512,1152]{1,0:T(8,128)(2,1)}, u32[]{:S(2)}) copy-start(bf16[512,1152]{1,0:T(8,128)(2,1)} %copy-done.2) | copy-start | bytes 3538948
  68.1 6.8 %copy-start.7 = (bf16[512,1152]{1,0:T(8,128)(2,1)S(1)}, bf16[512,1152]{1,0:T(8,128)(2,1)}, u32[]{:S(2)}) copy-start(bf16[512,1152]{1,0:T(8,128)(2,1)} %copy-done.5) | copy-start | bytes 3538948
  74.1 13.4 %collective-permute-start.6 = (f32[128,1152]{1,0:T(8,128)S(1)}, f32[128,1152]{1,0:T(8,128)S(1)}, u32[]{:S(2)}, u32[]{:S(2)}) collective-permute-start(f32[128,1152]{1,0:T(8,128)S(1)} %get-tuple-element.95), channel_id=1, source_target_pairs={{0,128},{16,16},{32,32},{48,48},{64,64},{80,80},{96,96},{112,112},... | collective-permute-start | bytes 1769480 | tf_op jit(solution)/shard_map/ppermute | solution.py:179
  74.8 19.3 %collective-permute-start.9 = (f32[128,1152]{1,0:T(8,128)S(1)}, f32[128,1152]{1,0:T(8,128)S(1)}, u32[]{:S(2)}, u32[]{:S(2)}) collective-permute-start(f32[128,1152]{1,0:T(8,128)S(1)} %get-tuple-element.104), channel_id=1, source_target_pairs={{0,240},{16,0},{32,16},{48,32},{64,48},{80,64},{96,80},{112,96},{1... | collective-permute-start | bytes 1769480 | tf_op jit(solution)/shard_map/ppermute | solution.py:173
  81.4 25.9 %collective-permute-start.10 = (f32[256,1152]{1,0:T(8,128)S(1)}, f32[256,1152]{1,0:T(8,128)S(1)}, u32[]{:S(2)}, u32[]{:S(2)}) collective-permute-start(f32[256,1152]{1,0:T(8,128)S(1)} %get-tuple-element.107), channel_id=1, source_target_pairs={{0,1},{1,2},{2,3},{3,4},{4,5},{5,6},{6,7},{7,8},{8,9},{9,10},{10,1... | collective-permute-start | bytes 3538952 | tf_op jit(solution)/shard_map/ppermute | solution.py:173
  81.5 38.4 %collective-permute-start.11 = (f32[256,1152]{1,0:T(8,128)S(1)}, f32[256,1152]{1,0:T(8,128)S(1)}, u32[]{:S(2)}, u32[]{:S(2)}) collective-permute-start(f32[256,1152]{1,0:T(8,128)S(1)} %get-tuple-element.109), channel_id=1, source_target_pairs={{0,1},{1,2},{2,3},{3,4},{4,5},{5,6},{6,7},{7,8},{8,9},{9,10},{10,1... | collective-permute-start | bytes 3538952 | tf_op jit(solution)/shard_map/ppermute | solution.py:173
  84.4 21.5 %collective-permute-start.8 = (f32[128,1152]{1,0:T(8,128)S(1)}, f32[128,1152]{1,0:T(8,128)S(1)}, u32[]{:S(2)}, u32[]{:S(2)}) collective-permute-start(f32[128,1152]{1,0:T(8,128)S(1)} %collective-permute-done.4), channel_id=1, source_target_pairs={{0,112},{16,0},{32,16},{48,32},{64,48},{80,64},{96,80},{112,96},{1... | collective-permute-start | bytes 1769480 | tf_op jit(solution)/shard_map/ppermute | solution.py:202
  87.5 29.2 %collective-permute-start.7 = (f32[128,1152]{1,0:T(8,128)S(1)}, f32[128,1152]{1,0:T(8,128)S(1)}, u32[]{:S(2)}, u32[]{:S(2)}) collective-permute-start(f32[128,1152]{1,0:T(8,128)S(1)} %collective-permute-done.6), channel_id=1, source_target_pairs={{0,112},{16,0},{32,16},{48,32},{64,48},{80,64},{96,80},{112,96},{1... | collective-permute-start | bytes 1769480 | tf_op jit(solution)/shard_map/ppermute | solution.py:202

commit v4 on v3

--- a/solution.py
+++ b/solution.py
@@ -217,13 +217,12 @@
     work = 6 * rows * rows * width
     text_next = shifted(texts, "inner", -1)
     other = exchanged(images)
-    ih, il, th, tl = call(split_kernel, [half] * 4, [scale, bias, images, texts], {}, 0)
-    other, images, ih = tied(other, images, ih)
     half_outer = lax.axis_size("outer") // 2
     edge = lax.axis_index("outer") % half_outer == half_outer - 1
     take = jnp.logical_and(edge, lax.axis_index("inner") % 2 == 0)
     first = jnp.where(take, other[:size], images[:size])
-    first, images, other = tied(first, images, other)
+    first, images, other, texts = tied(first, images, other, texts)
+    ih, il, th, tl = call(split_kernel, [half] * 4, [scale, bias, images, texts], {}, 0)
     last = jnp.where(take, other[size:], images[size:])
     last, ih = tied(last, ih)
     first, last = advanced(first), advanced(last)

time: 123 us -> 122 us (level)
  local copies, waits for them, and re-layouts: 9.59 us -> 7.93 us
  starting transfers between devices: 15 us -> 16.4 us
    ppermute x2, waiting for transfers between devices: 9.93 us -> 0.01 us  [advanced(): return lax.ppermute(array, ('outer', 'inner'), pairs)]
    ppermute x1, waiting for transfers between devices: 17.5 us -> 22.7 us  [exchanged(): return lax.ppermute(array, ('outer', 'inner'), pairs)]
    ppermute x5, starting transfers between devices: 6.89 us -> 11.2 us  [shifted(): lax.ppermute(array, axis, [(i, (i + by) % size) for i in range(size)])]
    ppermute x5, waiting for transfers between devices: 4.45 us -> 7.69 us  [shifted(): lax.ppermute(array, axis, [(i, (i + by) % size) for i in range(size)])]
    ppermute x2, starting transfers between devices: 3.18 us -> 0.15 us  [turned(): return lax.ppermute(array, 'outer', pairs)]
    unnamed x30, local copies, waits for them, and re-layouts: 9.45 us -> 7.79 us
  transfers between devices with their start and end apart: 12 -> 12, of which waited for: 8 -> 5; matrix products, arithmetic and copies ran while one was open for 4% -> 5% of each run, Pallas kernels for 31% -> 31%
where the time goes in v4:
time: 122 us; the launch traced here: 121 us
  waiting for transfers between devices  50 us (41%)
  Pallas kernels  38.5 us (32%)
  starting transfers between devices  16.4 us (13%)
  local copies, waits for them, and re-layouts  7.93 us (6%)
  other arithmetic  6.14 us (5%)
  between operations  2.36 us (2%)
    pallas_call x8, Pallas kernels, call(): pl.pallas_call(kernel, out_shape=[jax.ShapeDtypeStruct(s, d) for s, d in...  33.5 us
    ppermute x1, waiting for transfers between devices, exchanged(): return lax.ppermute(array, ('outer', 'inner'), pairs)  22.7 us
    ppermute x2, waiting for transfers between devices, turned(): return lax.ppermute(array, 'outer', pairs)  19.6 us
    ppermute x5, starting transfers between devices, shifted(): lax.ppermute(array, axis, [(i, (i + by) % size) for i in range(size)])  11.2 us
    unnamed x30, local copies, waits for them, and re-layouts  7.79 us
    ppermute x5, waiting for transfers between devices, shifted(): lax.ppermute(array, axis, [(i, (i + by) % size) for i in range(size)])  7.69 us
    pallas_call x5, Pallas kernels, place(): pl.pallas_call(functools.partial(place_kernel, start), out_shape=jax.Shap...  4.93 us
    ppermute x1, starting transfers between devices, exchanged(): return lax.ppermute(array, ('outer', 'inner'), pairs)  3.4 us
  transfers between devices with their start and end apart: 12, of which 5 were waited for; matrix products, arithmetic and copies ran while one was open for 5% of the time, Pallas kernels for 31%

profile of v4, /device:TPU:224, one launch (start us, length us, event | category | flops | bytes accessed | tf_op | source)
XLA Modules:
  0.0 121.3 jit_solution(16191077124746238652)
XLA Ops:
  0.6 3.4 %collective-permute-start = (f32[512,1152]{1,0:T(8,128)}, f32[512,1152]{1,0:T(8,128)}, u32[]{:S(2)}, u32[]{:S(2)}) collective-permute-start(f32[512,1152]{1,0:T(8,128)} %images), channel_id=1, source_target_pairs={{112,240},{114,242},{116,244},{118,246},{120,248},{122,250},{124,2... | collective-permute-start | bytes 7077896 | tf_op jit(solution)/shard_map/ppermute | solution.py:186
  4.0 3.6 %collective-permute-start.2 = (f32[512,1152]{1,0:T(8,128)}, f32[512,1152]{1,0:T(8,128)S(1)}, u32[]{:S(2)}, u32[]{:S(2)}) collective-permute-start(f32[512,1152]{1,0:T(8,128)} %texts), channel_id=1, source_target_pairs={{0,15},{1,0},{2,1},{3,2},{4,3},{5,4},{6,5},{7,6},{8,7},{9,8},{10,9... | collective-permute-start | bytes 7077896 | tf_op jit(solution)/shard_map/ppermute | solution.py:173
  8.9 22.7 %collective-permute-done = f32[512,1152]{1,0:T(8,128)} collective-permute-done((f32[512,1152]{1,0:T(8,128)}, f32[512,1152]{1,0:T(8,128)}, u32[]{:S(2)}, u32[]{:S(2)}) %collective-permute-start) | collective-permute-done | bytes 2359328 | tf_op jit(solution)/shard_map/ppermute | solution.py:186
  31.7 2.8 %slice_select_fusion = f32[256,1152]{1,0:T(8,128)} fusion(f32[512,1152]{1,0:T(8,128)} %collective-permute-done, f32[512,1152]{1,0:T(8,128)} %images, pred[]{:T(512)S(6)} %and.16), kind=kLoop, calls=%fused_computation | loop fusion | flops 294912 | bytes 3538945 | tf_op jit(solution)/shard_map/jit(_where)/select_n | solution.py:223
  34.5 1.7 %copy-done.1 = f32[512,1152]{1,0:T(8,128)S(1)} copy-done((f32[512,1152]{1,0:T(8,128)S(1)}, f32[512,1152]{1,0:T(8,128)}, u32[]{:S(2)}) %copy-start.1) | copy-done | bytes 2359320
  36.2 0.9 shard_map.68
  37.0 1.0 copy-done.11
  38.1 3.3 %slice_select_fusion.1 = f32[256,1152]{1,0:T(8,128)} fusion(f32[512,1152]{1,0:T(8,128)S(1)} %copy-done, f32[512,1152]{1,0:T(8,128)} %collective-permute-done, pred[]{:T(512)S(6)} %and.16), kind=kLoop, calls=%fused_computation.1 | loop fusion | flops 294912 | bytes 3538945 | tf_op jit(solution)/shard_map/jit(_where)/select_n | solution.py:226
  41.8 1.3 %copy-done.3 = bf16[512,1152]{1,0:T(8,128)(2,1)S(1)} copy-done((bf16[512,1152]{1,0:T(8,128)(2,1)S(1)}, bf16[512,1152]{1,0:T(8,128)(2,1)}, u32[]{:S(2)}) %copy-start.3) | copy-done | bytes 1179672
  43.1 1.3 %copy-done.6 = bf16[512,1152]{1,0:T(8,128)(2,1)S(1)} copy-done((bf16[512,1152]{1,0:T(8,128)(2,1)S(1)}, bf16[512,1152]{1,0:T(8,128)(2,1)}, u32[]{:S(2)}) %copy-start.6) | copy-done | bytes 1179672
  44.4 1.3 %copy-done.9 = bf16[512,1152]{1,0:T(8,128)(2,1)S(1)} copy-done((bf16[512,1152]{1,0:T(8,128)(2,1)S(1)}, bf16[512,1152]{1,0:T(8,128)(2,1)}, u32[]{:S(2)}) %copy-start.9) | copy-done | bytes 1179672
  45.7 1.3 %copy-done.12 = bf16[512,1152]{1,0:T(8,128)(2,1)S(1)} copy-done((bf16[512,1152]{1,0:T(8,128)(2,1)S(1)}, bf16[512,1152]{1,0:T(8,128)(2,1)}, u32[]{:S(2)}) %copy-start.12) | copy-done | bytes 1179672
  46.9 8.7 %shard_map.69 = (f32[512,1152]{1,0:T(8,128)S(1)}, f32[512,1152]{1,0:T(8,128)S(1)}) custom-call(f32[1]{0:T(128)S(6)} %copy.16.scale_ref, f32[1]{0:T(128)S(6)} %copy.17.bias_ref, bf16[512,1152]{1,0:T(8,128)(2,1)S(1)} %copy-done.3, bf16[512,1152]{1,0:T(8,128)(2,1)S(1)} %copy-done.6, bf16[512,1152]{1,0:T(8,128)(2,1)S(1)} %copy-done.9, ...), custom_call_target="tpu_custom_call" | custom-call | flops 5435817984 | bytes 1048576 | tf_op jit(solution)/shard_map/pallas_call | solution.py:159
  55.7 3.7 %shard_map.70 = (bf16[256,1152]{1,0:T(8,128)(2,1)S(1)}, bf16[256,1152]{1,0:T(8,128)(2,1)S(1)}, bf16[256,512]{1,0:T(8,128)(2,1)S(1)}, bf16[256,512]{1,0:T(8,128)(2,1)S(1)}, f32[256,1152]{1,0:T(8,128)S(1)}) custom-call(f32[1]{0:T(128)S(6)} %copy.16.scale_ref, f32[1]{0:T(128)S(6)} %copy.17.bias_ref, f32[256,1152]{1,0:T(8,128)} %collective-permute-done.1.piece, ...), custom_call_target="tpu_custom_call" | custom-call | flops 1811939328 | bytes 1048576 | tf_op jit(solution)/shard_map/pallas_call | solution.py:159
  59.4 2.8 %shard_map.71 = (f32[128,1152]{1,0:T(8,128)S(1)}, f32[128,1152]{1,0:T(8,128)S(1)}, bf16[256,512]{1,0:T(8,128)(2,1)S(1)}, bf16[256,512]{1,0:T(8,128)(2,1)S(1)}, b...) custom-call(f32[1]{0:T(128)S(6)} %copy.16.scale_ref, f32[1]{0:T(128)S(6)} %copy.17.bias_ref, ...), custom_call_target="tpu_custom_call" | custom-call | flops 1811939328 | bytes 1048576 | tf_op jit(solution)/shard_map/pallas_call | solution.py:159
  62.2 0.7 collective-permute-start.4
  62.9 2.3 %collective-permute-start.5 = (f32[128,1152]{1,0:T(8,128)S(1)}, f32[128,1152]{1,0:T(8,128)S(1)}, u32[]{:S(2)}, u32[]{:S(2)}) collective-permute-start(f32[128,1152]{1,0:T(8,128)S(1)} %get-tuple-element.83), channel_id=1, source_target_pairs={{0,240},{16,0},{32,16},{48,32},{64,48},{80,64},{96,80},{112,96},{1... | collective-permute-start | bytes 1769480 | tf_op jit(solution)/shard_map/ppermute | solution.py:173
  65.2 6.0 %shard_map.72 = (f32[128,1152]{1,0:T(8,128)S(1)}, f32[128,1152]{1,0:T(8,128)S(1)}, bf16[256,1152]{1,0:T(8,128)(2,1)S(1)}, bf16[256,1152]{1,0:T(8,128)(2,1)S(1)},...) custom-call(f32[1]{0:T(128)S(6)} %copy.16.scale_ref, ...), custom_call_target="tpu_custom_call" | custom-call | flops 3623878656 | bytes 1048576 | tf_op jit(solution)/shard_map/pallas_call | solution.py:159
  71.9 2.1 %collective-permute-start.9 = (f32[128,1152]{1,0:T(8,128)S(1)}, f32[128,1152]{1,0:T(8,128)S(1)}, u32[]{:S(2)}, u32[]{:S(2)}) collective-permute-start(f32[128,1152]{1,0:T(8,128)S(1)} %get-tuple-element.100), channel_id=1, source_target_pairs={{0,240},{16,0},{32,16},{48,32},{64,48},{80,64},{96,80},{112,96},{1... | collective-permute-start | bytes 1769480 | tf_op jit(solution)/shard_map/ppermute | solution.py:173
  74.0 6.5 %shard_map.73 = (f32[256,1152]{1,0:T(8,128)S(1)}, f32[256,1152]{1,0:T(8,128)S(1)}, bf16[512,512]{1,0:T(8,128)(2,1)S(1)}, bf16[512,512]{1,0:T(8,128)(2,1)S(1)}) custom-call(f32[1]{0:T(128)S(6)} %copy.16.scale_ref, f32[1]{0:T(128)S(6)} %copy.17.bias_ref, bf16[512,1152]{1,0:T(8,128)(2,1)S(1)} %copy-done.4, bf16[512,1152]{1,0:T(8,128)(2,1)S(1)} %copy-done.7, ...), custom_call_target="tpu_custom_call" | custom-call | flops 5435817984 | bytes 1048576 | tf_op jit(solution)/shard_map/pallas_call | solution.py:159
  80.5 3.1 %collective-permute-start.11 = (f32[256,1152]{1,0:T(8,128)S(1)}, f32[256,1152]{1,0:T(8,128)S(1)}, u32[]{:S(2)}, u32[]{:S(2)}) collective-permute-start(f32[256,1152]{1,0:T(8,128)S(1)} %get-tuple-element.105), channel_id=1, source_target_pairs={{0,1},{1,2},{2,3},{3,4},{4,5},{5,6},{6,7},{7,8},{8,9},{9,10},{10,1... | collective-permute-start | bytes 3538952 | tf_op jit(solution)/shard_map/ppermute | solution.py:173
  83.7 2.2 %shard_map.74 = (f32[256,1152]{1,0:T(8,128)S(1)}, f32[256,1152]{1,0:T(8,128)S(1)}) custom-call(f32[1]{0:T(128)S(6)} %copy.16.scale_ref, f32[1]{0:T(128)S(6)} %copy.17.bias_ref, f32[512,1152]{1,0:T(8,128)S(1)} %get-tuple-element.84.text_in, bf16[256,1152]{1,0:T(8,128)(2,1)S(1)} %get-tuple-element.68.ph.refs_0_, ...), custom_call_target="tpu_custom_call" | custom-call | flops 1811939328 | bytes 1048576 | tf_op jit(solution)/shard_map/pallas_call | solution.py:159
  86.1 2.8 %shard_map.75 = (f32[512,1152]{1,0:T(8,128)}, f32[128,1152]{1,0:T(8,128)S(1)}, f32[128,1152]{1,0:T(8,128)S(1)}, f32[128,1152]{1,0:T(8,128)S(1)}) custom-call(f32[1]{0:T(128)S(6)} %copy.16.scale_ref, f32[1]{0:T(128)S(6)} %copy.17.bias_ref, f32[512,1152]{1,0:T(8,128)S(1)} %get-tuple-element.65.grad_in, bf16[512,512]{1,0:T(8,128)(2,1)S(1)} %get-tuple-element.92.uh, ...), custom_call_target="tpu_custom_call" | custom-call | flops 72477573120 | bytes 1048576 | tf_op jit(solution)/shard_map/pallas_call | solution.py:159
  88.9 5.3 %collective-permute-done.9.back = f32[128,1152]{1,0:T(8,128)S(1)} collective-permute-done((f32[128,1152]{1,0:T(8,128)S(1)}, f32[128,1152]{1,0:T(8,128)S(1)}, u32[]{:S(2)}, u32[]{:S(2)}) %collective-permute-start.9) | collective-permute-done | bytes 589856 | tf_op jit(solution)/shard_map/ppermute | solution.py:173
  94.2 0.9 shard_map.76.refs_0_
  95.1 11.8 %collective-permute-done.8.back = f32[128,1152]{1,0:T(8,128)S(1)} collective-permute-done((f32[128,1152]{1,0:T(8,128)S(1)}, f32[128,1152]{1,0:T(8,128)S(1)}, u32[]{:S(2)}, u32[]{:S(2)}) %collective-permute-start.8) | collective-permute-done | bytes 589856 | tf_op jit(solution)/shard_map/ppermute | solution.py:202
  106.9 0.9 shard_map.77.refs_0_
  107.8 1.1 shard_map.78.refs_0_
  108.9 7.8 %collective-permute-done.7.back = f32[128,1152]{1,0:T(8,128)S(1)} collective-permute-done((f32[128,1152]{1,0:T(8,128)S(1)}, f32[128,1152]{1,0:T(8,128)S(1)}, u32[]{:S(2)}, u32[]{:S(2)}) %collective-permute-start.7) | collective-permute-done | bytes 589856 | tf_op jit(solution)/shard_map/ppermute | solution.py:202
  116.7 0.9 shard_map.79
  117.6 2.3 %collective-permute-done.11.back = f32[256,1152]{1,0:T(8,128)S(1)} collective-permute-done((f32[256,1152]{1,0:T(8,128)S(1)}, f32[256,1152]{1,0:T(8,128)S(1)}, u32[]{:S(2)}, u32[]{:S(2)}) %collective-permute-start.11) | collective-permute-done | bytes 1179680 | tf_op jit(solution)/shard_map/ppermute | solution.py:173
  120.0 1.1 shard_map.80
  (38 shorter events, 1.4 us)
Async XLA Ops:
  0.6 31.1 %collective-permute-start = (f32[512,1152]{1,0:T(8,128)}, f32[512,1152]{1,0:T(8,128)}, u32[]{:S(2)}, u32[]{:S(2)}) collective-permute-start(f32[512,1152]{1,0:T(8,128)} %images), channel_id=1, source_target_pairs={{112,240},{114,242},{116,244},{118,246},{120,248},{122,250},{124,2... | collective-permute-start | bytes 7077896 | tf_op jit(solution)/shard_map/ppermute | solution.py:186
  4.0 55.3 %collective-permute-start.2 = (f32[512,1152]{1,0:T(8,128)}, f32[512,1152]{1,0:T(8,128)S(1)}, u32[]{:S(2)}, u32[]{:S(2)}) collective-permute-start(f32[512,1152]{1,0:T(8,128)} %texts), channel_id=1, source_target_pairs={{0,15},{1,0},{2,1},{3,2},{4,3},{5,4},{6,5},{7,6},{8,7},{9,8},{10,9... | collective-permute-start | bytes 7077896 | tf_op jit(solution)/shard_map/ppermute | solution.py:173
  8.9 25.6 %copy-start = (f32[512,1152]{1,0:T(8,128)S(1)}, f32[512,1152]{1,0:T(8,128)}, u32[]{:S(2)}) copy-start(f32[512,1152]{1,0:T(8,128)} %images) | copy-start | bytes 7077892
  34.5 21.2 %collective-permute-start.1 = (f32[256,1152]{1,0:T(8,128)}, f32[256,1152]{1,0:T(8,128)}, u32[]{:S(2)}, u32[]{:S(2)}) collective-permute-start(f32[256,1152]{1,0:T(8,128)} %slice_select_fusion), channel_id=1, source_target_pairs={{0,16},{1,17},{2,18},{3,19},{4,20},{5,21},{6,22},{7,23},{8,24},{9,... | collective-permute-start | bytes 3538952 | tf_op jit(solution)/shard_map/ppermute | solution.py:196
  34.5 1.7 %copy-start.1 = (f32[512,1152]{1,0:T(8,128)S(1)}, f32[512,1152]{1,0:T(8,128)}, u32[]{:S(2)}) copy-start(f32[512,1152]{1,0:T(8,128)} %texts) | copy-start | bytes 7077892
  37.0 1.0 copy-start.11
  38.0 3.4 %copy-start.2 = (bf16[512,1152]{1,0:T(8,128)(2,1)}, bf16[512,1152]{1,0:T(8,128)(2,1)S(1)}, u32[]{:S(2)}) copy-start(bf16[512,1152]{1,0:T(8,128)(2,1)S(1)} %get-tuple-element.60.ih) | copy-start | bytes 3538948
  38.0 3.4 %copy-start.5 = (bf16[512,1152]{1,0:T(8,128)(2,1)}, bf16[512,1152]{1,0:T(8,128)(2,1)S(1)}, u32[]{:S(2)}) copy-start(bf16[512,1152]{1,0:T(8,128)(2,1)S(1)} %get-tuple-element.61.il) | copy-start | bytes 3538948
  38.0 3.4 %copy-start.8 = (bf16[512,1152]{1,0:T(8,128)(2,1)}, bf16[512,1152]{1,0:T(8,128)(2,1)S(1)}, u32[]{:S(2)}) copy-start(bf16[512,1152]{1,0:T(8,128)(2,1)S(1)} %get-tuple-element.67.th) | copy-start | bytes 3538948
  38.0 3.6 %copy-start.14 = (s32[1,512]{1,0:T(1,128)S(1)}, s32[1,512]{1,0:T(1,128)}, u32[]{:S(2)}) copy-start(s32[1,512]{1,0:T(1,128)} %param.7) | copy-start | bytes 6148
  41.4 23.8 %collective-permute-start.3 = (f32[256,1152]{1,0:T(8,128)}, f32[256,1152]{1,0:T(8,128)}, u32[]{:S(2)}, u32[]{:S(2)}) collective-permute-start(f32[256,1152]{1,0:T(8,128)} %slice_select_fusion.1), channel_id=1, source_target_pairs={{0,16},{1,17},{2,18},{3,19},{4,20},{5,21},{6,22},{7,23},{8,24},{9,... | collective-permute-start | bytes 3538952 | tf_op jit(solution)/shard_map/ppermute | solution.py:196
  41.8 1.3 %copy-start.3 = (bf16[512,1152]{1,0:T(8,128)(2,1)S(1)}, bf16[512,1152]{1,0:T(8,128)(2,1)}, u32[]{:S(2)}) copy-start(bf16[512,1152]{1,0:T(8,128)(2,1)} %copy-done.2) | copy-start | bytes 3538948
  43.1 1.3 %copy-start.6 = (bf16[512,1152]{1,0:T(8,128)(2,1)S(1)}, bf16[512,1152]{1,0:T(8,128)(2,1)}, u32[]{:S(2)}) copy-start(bf16[512,1152]{1,0:T(8,128)(2,1)} %copy-done.5) | copy-start | bytes 3538948
  44.4 1.3 %copy-start.9 = (bf16[512,1152]{1,0:T(8,128)(2,1)S(1)}, bf16[512,1152]{1,0:T(8,128)(2,1)}, u32[]{:S(2)}) copy-start(bf16[512,1152]{1,0:T(8,128)(2,1)} %copy-done.8) | copy-start | bytes 3538948
  45.7 1.3 %copy-start.12 = (bf16[512,1152]{1,0:T(8,128)(2,1)S(1)}, bf16[512,1152]{1,0:T(8,128)(2,1)}, u32[]{:S(2)}) copy-start(bf16[512,1152]{1,0:T(8,128)(2,1)} %copy-done.11) | copy-start | bytes 3538948
  46.9 8.7 %copy-start.10 = (bf16[512,1152]{1,0:T(8,128)(2,1)S(1)}, bf16[512,1152]{1,0:T(8,128)(2,1)}, u32[]{:S(2)}) copy-start(bf16[512,1152]{1,0:T(8,128)(2,1)} %copy-done.8) | copy-start | bytes 3538948
  46.9 8.7 %copy-start.13 = (bf16[512,1152]{1,0:T(8,128)(2,1)S(1)}, bf16[512,1152]{1,0:T(8,128)(2,1)}, u32[]{:S(2)}) copy-start(bf16[512,1152]{1,0:T(8,128)(2,1)} %copy-done.11) | copy-start | bytes 3538948
  62.2 18.4 %collective-permute-start.4 = (f32[128,1152]{1,0:T(8,128)S(1)}, f32[128,1152]{1,0:T(8,128)S(1)}, u32[]{:S(2)}, u32[]{:S(2)}) collective-permute-start(f32[128,1152]{1,0:T(8,128)S(1)} %get-tuple-element.82), channel_id=1, source_target_pairs={{0,128},{16,16},{32,32},{48,48},{64,64},{80,80},{96,96},{112,112},... | collective-permute-start | bytes 1769480 | tf_op jit(solution)/shard_map/ppermute | solution.py:179
  62.9 20.8 %collective-permute-start.5 = (f32[128,1152]{1,0:T(8,128)S(1)}, f32[128,1152]{1,0:T(8,128)S(1)}, u32[]{:S(2)}, u32[]{:S(2)}) collective-permute-start(f32[128,1152]{1,0:T(8,128)S(1)} %get-tuple-element.83), channel_id=1, source_target_pairs={{0,240},{16,0},{32,16},{48,32},{64,48},{80,64},{96,80},{112,96},{1... | collective-permute-start | bytes 1769480 | tf_op jit(solution)/shard_map/ppermute | solution.py:173
  65.2 8.8 %copy-start.4 = (bf16[512,1152]{1,0:T(8,128)(2,1)S(1)}, bf16[512,1152]{1,0:T(8,128)(2,1)}, u32[]{:S(2)}) copy-start(bf16[512,1152]{1,0:T(8,128)(2,1)} %copy-done.2) | copy-start | bytes 3538948
  65.2 8.8 %copy-start.7 = (bf16[512,1152]{1,0:T(8,128)(2,1)S(1)}, bf16[512,1152]{1,0:T(8,128)(2,1)}, u32[]{:S(2)}) copy-start(bf16[512,1152]{1,0:T(8,128)(2,1)} %copy-done.5) | copy-start | bytes 3538948
  71.2 14.8 %collective-permute-start.6 = (f32[128,1152]{1,0:T(8,128)S(1)}, f32[128,1152]{1,0:T(8,128)S(1)}, u32[]{:S(2)}, u32[]{:S(2)}) collective-permute-start(f32[128,1152]{1,0:T(8,128)S(1)} %get-tuple-element.91), channel_id=1, source_target_pairs={{0,128},{16,16},{32,32},{48,48},{64,64},{80,80},{96,96},{112,112},... | collective-permute-start | bytes 1769480 | tf_op jit(solution)/shard_map/ppermute | solution.py:179
  71.9 22.3 %collective-permute-start.9 = (f32[128,1152]{1,0:T(8,128)S(1)}, f32[128,1152]{1,0:T(8,128)S(1)}, u32[]{:S(2)}, u32[]{:S(2)}) collective-permute-start(f32[128,1152]{1,0:T(8,128)S(1)} %get-tuple-element.100), channel_id=1, source_target_pairs={{0,240},{16,0},{32,16},{48,32},{64,48},{80,64},{96,80},{112,96},{1... | collective-permute-start | bytes 1769480 | tf_op jit(solution)/shard_map/ppermute | solution.py:173
  80.4 27.3 %collective-permute-start.10 = (f32[256,1152]{1,0:T(8,128)S(1)}, f32[256,1152]{1,0:T(8,128)S(1)}, u32[]{:S(2)}, u32[]{:S(2)}) collective-permute-start(f32[256,1152]{1,0:T(8,128)S(1)} %get-tuple-element.103), channel_id=1, source_target_pairs={{0,1},{1,2},{2,3},{3,4},{4,5},{5,6},{6,7},{7,8},{8,9},{9,10},{10,1... | collective-permute-start | bytes 3538952 | tf_op jit(solution)/shard_map/ppermute | solution.py:173
  80.5 39.4 %collective-permute-start.11 = (f32[256,1152]{1,0:T(8,128)S(1)}, f32[256,1152]{1,0:T(8,128)S(1)}, u32[]{:S(2)}, u32[]{:S(2)}) collective-permute-start(f32[256,1152]{1,0:T(8,128)S(1)} %get-tuple-element.105), channel_id=1, source_target_pairs={{0,1},{1,2},{2,3},{3,4},{4,5},{5,6},{6,7},{7,8},{8,9},{9,10},{10,1... | collective-permute-start | bytes 3538952 | tf_op jit(solution)/shard_map/ppermute | solution.py:173
  83.7 23.2 %collective-permute-start.8 = (f32[128,1152]{1,0:T(8,128)S(1)}, f32[128,1152]{1,0:T(8,128)S(1)}, u32[]{:S(2)}, u32[]{:S(2)}) collective-permute-start(f32[128,1152]{1,0:T(8,128)S(1)} %collective-permute-done.4), channel_id=1, source_target_pairs={{0,112},{16,0},{32,16},{48,32},{64,48},{80,64},{96,80},{112,96},{1... | collective-permute-start | bytes 1769480 | tf_op jit(solution)/shard_map/ppermute | solution.py:202
  86.0 30.8 %collective-permute-start.7 = (f32[128,1152]{1,0:T(8,128)S(1)}, f32[128,1152]{1,0:T(8,128)S(1)}, u32[]{:S(2)}, u32[]{:S(2)}) collective-permute-start(f32[128,1152]{1,0:T(8,128)S(1)} %collective-permute-done.6), channel_id=1, source_target_pairs={{0,112},{16,0},{32,16},{48,32},{64,48},{80,64},{96,80},{112,96},{1... | collective-permute-start | bytes 1769480 | tf_op jit(solution)/shard_map/ppermute | solution.py:202
